TPU v7x, 256 devices: a whole 4x4x8 slice. The times are simulated.
256 devices in a mesh: band: 8 (over y, core), tile: 32 (over z, x).
Axes of the slice: x: 4, y: 4, z: 8, core: 2. Of those that a mesh axis runs over, the one named last changes fastest.
Arguments:
- right_side: float32 [16, 192, 4096], P(None, 'band', 'tile'), may hold values from -54 to 54
- coeff_field: float32 [192, 4096], P('band', 'tile'), may hold values from 0.25 to 4
- factor_blocks: bfloat16 [8, 32, 116, 128, 128], P('band', 'tile'), may hold values from -1 to 2, as said below
- block_rows: int32 [8, 32, 116], P('band', 'tile'), may hold values from 0 to 28, as said below
- block_cols: int32 [8, 32, 116], P('band', 'tile'), may hold values from 0 to 28, as said below
- prolong: float32 [192, 1, 128, 4096], P('band', None, None, 'tile'), may hold values from -0.3125 to 0.3125
- coarse_picks: int32 [192, 32, 1], P('band', 'tile'), may hold values from 0 to 3
- coarse_factor: float32 [8, 512, 512], P('band'), may hold values from -1 to 1, as said below
Outputs:
- solution: float32 [16, 192, 4096], P(None, 'band', 'tile')
- residual: float32 [16, 192, 4096], P(None, 'band', 'tile')
- precond: float32 [16, 192, 4096], P(None, 'band', 'tile')
Inputs may be any that keep to these rules, and one draw needn't show every extreme that they name: `block_rows`: entry k < 29 of a subdomain's list is k; every later entry is a tile row of 1 to 28. `block_cols`: entry k < 29 is k, so that tile (k, k) is stored first; every later entry is below its block_rows entry. `factor_blocks`: stored tile k < 29 of a subdomain is its diagonal tile: lower triangular with diagonal entries of 1 to 2. `coarse_factor`: lower triangular, diagonal entries of 0.6 to 1.0. `coarse_picks`: the 1 slots of a row name different blocks.
All inputs are finite; a program needn't handle non-finite values.
Results may differ from a plain program's by a relative error of at most 0.018.
Values may be sent and summed in bfloat16 or wider, within the bound.
A program may use at most 64 MiB of HBM per device.

v0:
```python
import jax
import jax.numpy as jnp
from jax import lax
from jax.sharding import PartitionSpec as P

W = 2
NCB = 4
ITERS = 3


highest = lax.Precision.HIGHEST


def padded_2(cells, sides, width):
    for axis, dim in sides:
        count = lax.axis_size(axis)
        ends = count - 1
        head = lax.slice_in_dim(cells, 0, width, axis=dim)
        tail = lax.slice_in_dim(cells, cells.shape[dim] - width, cells.shape[dim], axis=dim)
        cells = jnp.concatenate(
            [
                lax.ppermute(tail, axis, [(i, (i + 1) % count) for i in range(ends)]),
                cells,
                lax.ppermute(head, axis, [((i + 1) % count, i) for i in range(ends)]),
            ],
            axis=dim,
        )
    return cells


def stencil(padded, coeff):
    center = padded[:, 1:-1, 1:-1]
    beside_all = (
        padded[:, :-2, 1:-1] + padded[:, 2:, 1:-1] + padded[:, 1:-1, :-2] + padded[:, 1:-1, 2:]
    )
    return 0.25 * ((coeff + 4.0) * center - beside_all)


def block_solve(extended, factor, rows_idx, cols_idx):
    columns, ext_rows, ext_cols = extended.shape
    node_count = ext_rows * ext_cols
    tile_size = factor.shape[-1]
    block_count = factor.shape[0]
    tile_count = (node_count + tile_size - 1) // tile_size
    flattened = jnp.pad(
        extended.reshape(columns, node_count), ((0, 0), (0, tile_count * tile_size - node_count))
    )
    pieces = flattened.reshape(columns, tile_count, tile_size).transpose(1, 0, 2)
    places = jnp.arange(tile_count, dtype=jnp.int32)[:, None]
    place_rows = (rows_idx[None, :] == places).astype(jnp.float32)
    place_cols = (cols_idx[None, :] == places).astype(jnp.float32)
    inner_part = jnp.einsum(
        "bij,bcj->bci", factor, pieces[cols_idx], preferred_element_type=jnp.float32
    )
    gathered = jnp.dot(place_rows, inner_part.reshape(block_count, -1), precision=highest)
    gathered = gathered.astype(jnp.bfloat16).reshape(tile_count, columns, tile_size)
    outer_part = jnp.einsum(
        "bij,bci->bcj", factor, gathered[rows_idx], preferred_element_type=jnp.float32
    )
    spread = jnp.dot(place_cols, outer_part.reshape(block_count, -1), precision=highest)
    spread = (
        spread.reshape(tile_count, columns, tile_size)
        .transpose(1, 0, 2)
        .reshape(columns, tile_count * tile_size)
    )
    return spread[:, :node_count].reshape(columns, ext_rows, ext_cols)


def fold_margin(values, along, length, margin):
    middle = lax.slice_in_dim(values, 2 * margin, 2 * margin + length, axis=along)
    leading = lax.slice_in_dim(values, 0, margin, axis=along)
    trailing = lax.slice_in_dim(
        values, values.shape[along] - margin, values.shape[along], axis=along
    )
    filler_shape = list(leading.shape)
    filler_shape[along] = length - margin
    filler = jnp.zeros(tuple(filler_shape), values.dtype)
    return (
        middle
        + jnp.concatenate([leading, filler], along)
        + jnp.concatenate([filler, trailing], along)
    )


def local(
    right_side,
    coeff_field,
    factor_blocks,
    block_rows,
    block_cols,
    prolong,
    coarse_picks,
    coarse_factor,
):
    columns, own_rows, own_cols = right_side.shape
    factor = factor_blocks[0, 0]
    rows_idx = block_rows[0, 0]
    cols_idx = block_cols[0, 0]
    coarse_lower = coarse_factor[0]
    picks_here = coarse_picks[:, 0, :]
    block_len = prolong.shape[2]
    choose = (picks_here[:, :, None] == jnp.arange(NCB, dtype=jnp.int32)[None, None, :]).astype(
        jnp.float32
    )

    def restrict(field):
        partial_value = jnp.einsum("rksl,crl->crks", prolong, field, precision=highest)
        return jnp.einsum("crks,rkn->cns", partial_value, choose, precision=highest).reshape(
            columns, NCB * block_len
        )

    def lift(solved):
        picked = jnp.einsum(
            "rkn,cns->crks", choose, solved.reshape(columns, NCB, block_len), precision=highest
        )
        return jnp.einsum("rksl,crks->crl", prolong, picked, precision=highest)

    def coarse_solve(coarse_in):
        halfway = jnp.dot(coarse_in, coarse_lower.T, precision=highest)
        return jnp.dot(halfway, coarse_lower, precision=highest)

    def extend_residual(field):
        return padded_2(field.astype(jnp.bfloat16), (("band", 1), ("tile", 2)), W)

    def precondition(extended, field, coarse_given):
        spread = block_solve(extended, factor, rows_idx, cols_idx)
        coarse_given = lax.psum(restrict(field), "tile")
        lifted = lift(coarse_solve(coarse_given))
        depth = W
        padded = padded_2(spread, (("band", 1), ("tile", 2)), depth)
        local_part = fold_margin(fold_margin(padded, 1, own_rows, W), 2, own_cols, W)
        return (local_part + lifted, None, coarse_given)

    def global_dot(products):
        return lax.psum(products, ("band", "tile"))

    def edge_rim(field):
        return padded_2(field, (("band", 1), ("tile", 2)), 1)

    solution = jnp.zeros_like(right_side)
    residual = right_side
    extended = extend_residual(right_side)
    precond, precond_ext, coarse_now = precondition(extended, residual, None)
    precond_dot = global_dot(jnp.sum(residual * precond, axis=(1, 2)))
    search, search_ext = (precond, precond_ext)
    for iteration in range(ITERS):
        first_k = stencil(edge_rim(search), coeff_field)
        image = stencil(edge_rim(first_k), coeff_field)
        local_curv = jnp.sum(search * image, axis=(1, 2))
        curvature = lax.psum(local_curv, ("band", "tile"))
        step_size = precond_dot / curvature
        solution = solution + step_size[:, None, None] * search
        residual = residual - step_size[:, None, None] * image
        extended = extend_residual(residual)
        coarse_given = None
        precond, precond_ext, coarse_now = precondition(extended, residual, coarse_given)
        if iteration + 1 < ITERS:
            dot_next = global_dot(jnp.sum(residual * precond, axis=(1, 2)))
            ratio = dot_next / precond_dot
            search = precond + ratio[:, None, None] * search
            precond_dot = dot_next
    return (solution, residual, precond)


def solution(mesh):
    in_specs = (
        P(None, "band", "tile"),
        P("band", "tile"),
        P("band", "tile", None, None, None),
        P("band", "tile", None),
        P("band", "tile", None),
        P("band", None, None, "tile"),
        P("band", "tile", None),
        P("band", None, None),
    )
    out_specs = (P(None, "band", "tile"), P(None, "band", "tile"), P(None, "band", "tile"))
    return jax.shard_map(local, mesh=mesh, in_specs=in_specs, out_specs=out_specs, check_vma=False)
```

profile of v0, /device:TPU:1, one launch (start us, length us, event | category | flops | bytes accessed | tf_op | source)
XLA Modules:
  0.0 1325.2 jit_solution(17885861713292437655)
XLA Ops:
  1.7 4.6 collective-permute-start
  9.6 3.5 fusion.32
  14.0 117.8 %psum.70 = f32[16,512]{1,0:T(8,128)S(1)} all-reduce(f32[16,512]{1,0:T(8,128)S(1)} %bitcast.393), channel_id=1, replica_groups=mesh['band'=8,'tile'=32] {'tile'}, use_global_device_ids=true, to_apply=%region_0.1 | all-reduce | flops 8192 | bytes 65536 | tf_op jit(solution)/shard_map/psum | solution.py:127
  137.4 4.1 collective-permute-done.3
  142.8 4.1 fusion.14
  148.6 3.2 fusion.12
  153.6 32.4 %collective-permute-start.4 = (f32[16,2,132]{2,0,1:T(8,128)S(1)}, f32[16,2,132]{2,0,1:T(8,128)S(1)}, u32[]{:S(2)}, u32[]{:S(2)}) collective-permute-start(f32[16,2,132]{2,0,1:T(8,128)S(1)} %get-tuple-element.51), channel_id=1, source_target_pairs={{0,32},{32,64},{64,96},{96,128},{128,160},{160,192},{192,224},{1,3... | collective-permute-start | bytes 50696 | tf_op jit(solution)/shard_map/ppermute | solution.py:22
  188.9 3.0 collective-permute-done.5
  195.0 2.7 collective-permute-done.6
  197.7 4.1 collective-permute-done.7
  203.8 4.3 collective-permute-start.8
  210.0 3.0 collective-permute-done.9
  218.8 4.4 collective-permute-done.11
  223.5 4.1 collective-permute-start.12
  229.5 3.0 collective-permute-done.13
  232.7 3.7 collective-permute-start.14
  240.1 4.1 collective-permute-done.15
  244.5 86.2 %all-reduce.12 = (f32[16]{0:T(128)S(1)}, f32[16]{0:T(128)S(1)}) all-reduce(f32[16]{0:T(128)S(1)} %get-tuple-element.10, f32[16]{0:T(128)S(1)} %get-tuple-element.9), channel_id=1, replica_groups=mesh['band'=8,'tile'=32] {'band','tile'}, use_global_device_ids=true, to_apply=%region_2.3 | all-reduce | flops 32 | bytes 256 | tf_op jit(solution)/shard_map/psum | solution.py:135
  335.7 2.5 fusion.41
  338.5 111.5 %psum.73 = f32[16,512]{1,0:T(8,128)S(1)} all-reduce(f32[16,512]{1,0:T(8,128)S(1)} %bitcast.394), channel_id=1, replica_groups=mesh['band'=8,'tile'=32] {'tile'}, use_global_device_ids=true, to_apply=%region_5.6 | all-reduce | flops 8192 | bytes 65536 | tf_op jit(solution)/shard_map/psum | solution.py:127
  455.5 3.0 collective-permute-done.19
  461.4 4.3 fusion.10
  468.2 3.3 fusion.8
  475.0 32.1 %collective-permute-start.20 = (f32[16,2,132]{2,0,1:T(8,128)S(1)}, f32[16,2,132]{2,0,1:T(8,128)S(1)}, u32[]{:S(2)}, u32[]{:S(2)}) collective-permute-start(f32[16,2,132]{2,0,1:T(8,128)S(1)} %get-tuple-element.49), channel_id=1, source_target_pairs={{0,32},{32,64},{64,96},{96,128},{128,160},{160,192},{192,224},{1,3... | collective-permute-start | bytes 50696 | tf_op jit(solution)/shard_map/ppermute | solution.py:22
  510.7 3.0 collective-permute-done.21
  516.9 2.6 collective-permute-done.22
  519.5 4.1 collective-permute-done.23
  527.0 83.6 %psum.74 = f32[16]{0:T(128)S(1)} all-reduce(f32[16]{0:T(128)S(1)} %get-tuple-element.94), channel_id=1, replica_groups=mesh['band'=8,'tile'=32] {'band','tile'}, use_global_device_ids=true, to_apply=%region_7.8 | all-reduce | flops 16 | bytes 128 | tf_op jit(solution)/shard_map/psum | solution.py:135
  611.7 3.1 collective-permute-start.24
  616.7 3.0 collective-permute-done.25
  622.6 2.8 collective-permute-done.26
  625.4 4.1 collective-permute-done.27
  629.8 3.3 collective-permute-start.28
  635.0 3.0 collective-permute-done.29
  638.2 3.4 collective-permute-start.30
  645.3 4.1 collective-permute-done.31
  649.7 81.4 %psum.75 = f32[16]{0:T(128)S(1)} all-reduce(f32[16]{0:T(128)S(1)} %get-tuple-element.25), channel_id=1, replica_groups=mesh['band'=8,'tile'=32] {'band','tile'}, use_global_device_ids=true, to_apply=%region_9.10 | all-reduce | flops 16 | bytes 128 | tf_op jit(solution)/shard_map/psum | solution.py:150
  732.4 2.7 collective-permute-start.32
  737.0 2.5 fusion.50
  739.8 111.1 %psum.76 = f32[16,512]{1,0:T(8,128)S(1)} all-reduce(f32[16,512]{1,0:T(8,128)S(1)} %bitcast.395), channel_id=1, replica_groups=mesh['band'=8,'tile'=32] {'tile'}, use_global_device_ids=true, to_apply=%region_10.11 | all-reduce | flops 8192 | bytes 65536 | tf_op jit(solution)/shard_map/psum | solution.py:127
  855.5 2.5 collective-permute-done.35
  860.1 4.3 fusion.6
  866.9 3.3 fusion.4
  873.7 32.4 %collective-permute-start.36 = (f32[16,2,132]{2,0,1:T(8,128)S(1)}, f32[16,2,132]{2,0,1:T(8,128)S(1)}, u32[]{:S(2)}, u32[]{:S(2)}) collective-permute-start(f32[16,2,132]{2,0,1:T(8,128)S(1)} %get-tuple-element.47), channel_id=1, source_target_pairs={{0,32},{32,64},{64,96},{96,128},{128,160},{160,192},{192,224},{1,3... | collective-permute-start | bytes 50696 | tf_op jit(solution)/shard_map/ppermute | solution.py:22
  909.7 3.0 collective-permute-done.37
  915.8 2.8 collective-permute-done.38
  918.6 4.1 collective-permute-done.39
  926.1 85.1 %psum.77 = f32[16]{0:T(128)S(1)} all-reduce(f32[16]{0:T(128)S(1)} %get-tuple-element.96), channel_id=1, replica_groups=mesh['band'=8,'tile'=32] {'band','tile'}, use_global_device_ids=true, to_apply=%region_12.13 | all-reduce | flops 16 | bytes 128 | tf_op jit(solution)/shard_map/psum | solution.py:135
  1016.6 2.8 collective-permute-done.41
  1025.2 4.1 collective-permute-done.43
  1029.6 4.5 collective-permute-start.44
  1036.0 3.0 collective-permute-done.45
  1039.2 2.4 collective-permute-start.46
  1045.2 4.1 collective-permute-done.47
  1050.4 82.4 %psum.78 = f32[16]{0:T(128)S(1)} all-reduce(f32[16]{0:T(128)S(1)} %get-tuple-element.17), channel_id=1, replica_groups=mesh['band'=8,'tile'=32] {'band','tile'}, use_global_device_ids=true, to_apply=%region_14.15 | all-reduce | flops 16 | bytes 128 | tf_op jit(solution)/shard_map/psum | solution.py:150
  1136.3 2.7 collective-permute-start.49
  1139.0 2.5 fusion.59
  1141.8 111.5 %psum.79 = f32[16,512]{1,0:T(8,128)S(1)} all-reduce(f32[16,512]{1,0:T(8,128)S(1)} %bitcast.396), channel_id=1, replica_groups=mesh['band'=8,'tile'=32] {'tile'}, use_global_device_ids=true, to_apply=%region_15.16 | all-reduce | flops 8192 | bytes 65536 | tf_op jit(solution)/shard_map/psum | solution.py:127
  1257.6 3.9 collective-permute-done.51
  1263.7 4.1 fusion.2
  1269.6 3.2 fusion
  1274.6 32.1 %collective-permute-start.52 = (f32[16,2,132]{2,0,1:T(8,128)S(1)}, f32[16,2,132]{2,0,1:T(8,128)S(1)}, u32[]{:S(2)}, u32[]{:S(2)}) collective-permute-start(f32[16,2,132]{2,0,1:T(8,128)S(1)} %get-tuple-element.45), channel_id=1, source_target_pairs={{0,32},{32,64},{64,96},{96,128},{128,160},{160,192},{192,224},{1,3... | collective-permute-start | bytes 50696 | tf_op jit(solution)/shard_map/ppermute | solution.py:22
  1309.1 3.0 collective-permute-done.53
  1318.0 4.1 collective-permute-done.55
  (321 shorter events, 147.0 us)
Async XLA Ops:
  1.7 132.2 %collective-permute-start = (bf16[16,2,128]{2,1,0:T(2,128)(2,1)S(1)}, bf16[16,2,128]{2,1,0:T(2,128)(2,1)S(1)}, u32[]{:S(2)}, u32[]{:S(2)}) collective-permute-start(bf16[16,2,128]{2,1,0:T(2,128)(2,1)S(1)} %get-tuple-element.90), channel_id=1, source_target_pairs={{0,32},{32,64},{64,96},{96,128},{128,160},{160,192},{192,224},{1,3... | collective-permute-start | bytes 24584 | tf_op jit(solution)/shard_map/ppermute | solution.py:22
  6.3 127.6 %collective-permute-start.1 = (bf16[16,2,128]{2,1,0:T(2,128)(2,1)S(1)}, bf16[16,2,128]{2,1,0:T(2,128)(2,1)S(1)}, u32[]{:S(2)}, u32[]{:S(2)}) collective-permute-start(bf16[16,2,128]{2,1,0:T(2,128)(2,1)S(1)} %get-tuple-element.91), channel_id=1, source_target_pairs={{32,0},{64,32},{96,64},{128,96},{160,128},{192,160},{224,192},{33,... | collective-permute-start | bytes 24584 | tf_op jit(solution)/shard_map/ppermute | solution.py:24
  134.1 3.2 collective-permute-start.2
  135.4 6.0 collective-permute-start.3
  153.6 35.0 %collective-permute-start.4 = (f32[16,2,132]{2,0,1:T(8,128)S(1)}, f32[16,2,132]{2,0,1:T(8,128)S(1)}, u32[]{:S(2)}, u32[]{:S(2)}) collective-permute-start(f32[16,2,132]{2,0,1:T(8,128)S(1)} %get-tuple-element.51), channel_id=1, source_target_pairs={{0,32},{32,64},{64,96},{96,128},{128,160},{160,192},{192,224},{1,3... | collective-permute-start | bytes 50696 | tf_op jit(solution)/shard_map/ppermute | solution.py:22
  186.7 5.2 collective-permute-start.5
  192.0 5.7 collective-permute-start.6
  193.3 8.5 collective-permute-start.7
  203.8 6.2 collective-permute-start.8
  208.0 5.0 collective-permute-start.9
  213.2 5.7 collective-permute-start.10
  215.2 8.0 collective-permute-start.11
  216.5 114.7 %copy-start.8 = (f32[24,128]{1,0:T(8,128)}, f32[24,128]{1,0:T(8,128)S(1)}, u32[]{:S(2)}) copy-start(f32[24,128]{1,0:T(8,128)S(1)} %get-tuple-element.93) | copy-start | bytes 36868
  223.5 6.0 collective-permute-start.12
  227.6 5.0 collective-permute-start.13
  232.7 7.4 collective-permute-start.14
  236.5 7.7 collective-permute-start.15
  331.4 118.6 %collective-permute-start.16 = (bf16[16,2,128]{2,0,1:T(8,128)(2,1)S(1)}, bf16[16,2,128]{2,0,1:T(8,128)(2,1)S(1)}, u32[]{:S(2)}, u32[]{:S(2)}) collective-permute-start(bf16[16,2,128]{2,0,1:T(8,128)(2,1)S(1)} %get-tuple-element.88), channel_id=1, source_target_pairs={{0,32},{32,64},{64,96},{96,128},{128,160},{160,192},{192,224},{1,3... | collective-permute-start | bytes 24584 | tf_op jit(solution)/shard_map/ppermute | solution.py:22
  333.3 116.7 %collective-permute-start.17 = (bf16[16,2,128]{2,0,1:T(8,128)(2,1)S(1)}, bf16[16,2,128]{2,0,1:T(8,128)(2,1)S(1)}, u32[]{:S(2)}, u32[]{:S(2)}) collective-permute-start(bf16[16,2,128]{2,0,1:T(8,128)(2,1)S(1)} %get-tuple-element.89), channel_id=1, source_target_pairs={{32,0},{64,32},{96,64},{128,96},{160,128},{192,160},{224,192},{33,... | collective-permute-start | bytes 24584 | tf_op jit(solution)/shard_map/ppermute | solution.py:24
  451.3 4.2 collective-permute-start.18
  452.6 5.9 collective-permute-start.19
  475.0 35.4 %collective-permute-start.20 = (f32[16,2,132]{2,0,1:T(8,128)S(1)}, f32[16,2,132]{2,0,1:T(8,128)S(1)}, u32[]{:S(2)}, u32[]{:S(2)}) collective-permute-start(f32[16,2,132]{2,0,1:T(8,128)S(1)} %get-tuple-element.49), channel_id=1, source_target_pairs={{0,32},{32,64},{64,96},{96,128},{128,160},{160,192},{192,224},{1,3... | collective-permute-start | bytes 50696 | tf_op jit(solution)/shard_map/ppermute | solution.py:22
  508.5 5.2 collective-permute-start.21
  513.7 96.9 %copy-start.38 = (f32[16]{0:T(128)S(1)}, f32[16]{0:T(128)}, u32[]{:S(2)}) copy-start(f32[16]{0:T(128)} %copy-done.37) | copy-start | bytes 196
  513.8 5.7 collective-permute-start.22
  515.2 8.5 collective-permute-start.23
  523.9 105.6 %copy-start.9 = (f32[24,128]{1,0:T(8,128)S(1)}, f32[24,128]{1,0:T(8,128)}, u32[]{:S(2)}) copy-start(f32[24,128]{1,0:T(8,128)} %copy-done.8) | copy-start | bytes 36868
  611.7 5.0 collective-permute-start.24
  614.8 5.0 collective-permute-start.25
  619.9 5.5 collective-permute-start.26
  621.3 8.2 collective-permute-start.27
  629.8 5.2 collective-permute-start.28
  633.1 5.0 collective-permute-start.29
  638.2 7.0 collective-permute-start.30
  641.6 7.7 collective-permute-start.31
  732.4 118.5 %collective-permute-start.32 = (bf16[16,2,128]{2,0,1:T(8,128)(2,1)S(1)}, bf16[16,2,128]{2,0,1:T(8,128)(2,1)S(1)}, u32[]{:S(2)}, u32[]{:S(2)}) collective-permute-start(bf16[16,2,128]{2,0,1:T(8,128)(2,1)S(1)} %get-tuple-element.86), channel_id=1, source_target_pairs={{0,32},{32,64},{64,96},{96,128},{128,160},{160,192},{192,224},{1,3... | collective-permute-start | bytes 24584 | tf_op jit(solution)/shard_map/ppermute | solution.py:22
  735.1 115.9 %collective-permute-start.33 = (bf16[16,2,128]{2,0,1:T(8,128)(2,1)S(1)}, bf16[16,2,128]{2,0,1:T(8,128)(2,1)S(1)}, u32[]{:S(2)}, u32[]{:S(2)}) collective-permute-start(bf16[16,2,128]{2,0,1:T(8,128)(2,1)S(1)} %get-tuple-element.87), channel_id=1, source_target_pairs={{32,0},{64,32},{96,64},{128,96},{160,128},{192,160},{224,192},{33,... | collective-permute-start | bytes 24584 | tf_op jit(solution)/shard_map/ppermute | solution.py:24
  851.0 4.4 collective-permute-start.34
  852.3 5.6 collective-permute-start.35
  873.7 50.1 %copy-start.4 = (f32[16,24,128]{2,0,1:T(8,128)S(1)}, f32[16,24,128]{2,0,1:T(8,128)}, u32[]{:S(2)}) copy-start(f32[16,24,128]{2,0,1:T(8,128)} %copy-done.3) | copy-start | bytes 589828
  873.7 50.1 %copy-start.28 = (pred[128]{0:T(512)(128)(4,1)S(1)}, pred[128]{0:T(512)(128)(4,1)}, u32[]{:S(2)}) copy-start(pred[128]{0:T(512)(128)(4,1)} %constant.22.clone.1) | copy-start | bytes 388
  873.7 35.7 %collective-permute-start.36 = (f32[16,2,132]{2,0,1:T(8,128)S(1)}, f32[16,2,132]{2,0,1:T(8,128)S(1)}, u32[]{:S(2)}, u32[]{:S(2)}) collective-permute-start(f32[16,2,132]{2,0,1:T(8,128)S(1)} %get-tuple-element.47), channel_id=1, source_target_pairs={{0,32},{32,64},{64,96},{96,128},{128,160},{160,192},{192,224},{1,3... | collective-permute-start | bytes 50696 | tf_op jit(solution)/shard_map/ppermute | solution.py:22
  907.5 5.2 collective-permute-start.37
  912.7 98.5 %copy-start.36 = (f32[16]{0:T(128)S(1)}, f32[16]{0:T(128)}, u32[]{:S(2)}) copy-start(f32[16]{0:T(128)} %copy-done.35) | copy-start | bytes 196
  912.9 5.7 collective-permute-start.38
  914.2 8.5 collective-permute-start.39
  922.9 106.4 %copy-start.10 = (f32[24,128]{1,0:T(8,128)S(1)}, f32[24,128]{1,0:T(8,128)}, u32[]{:S(2)}) copy-start(f32[24,128]{1,0:T(8,128)} %copy-done.8) | copy-start | bytes 36868
  923.9 209.5 %copy-start.5 = (f32[16,24,128]{2,0,1:T(8,128)S(1)}, f32[16,24,128]{2,0,1:T(8,128)}, u32[]{:S(2)}) copy-start(f32[16,24,128]{2,0,1:T(8,128)} %copy-done.3) | copy-start | bytes 589828
  1012.2 4.3 collective-permute-start.40
  1014.4 5.0 collective-permute-start.41
  1019.5 5.7 collective-permute-start.42
  1021.6 7.7 collective-permute-start.43
  1029.6 6.4 collective-permute-start.44
  1034.1 5.0 collective-permute-start.45
  1039.2 6.0 collective-permute-start.46
  1041.6 7.7 collective-permute-start.47
  1134.4 119.9 %collective-permute-start.48 = (bf16[16,2,128]{2,0,1:T(8,128)(2,1)S(1)}, bf16[16,2,128]{2,0,1:T(8,128)(2,1)S(1)}, u32[]{:S(2)}, u32[]{:S(2)}) collective-permute-start(bf16[16,2,128]{2,0,1:T(8,128)(2,1)S(1)} %get-tuple-element.84), channel_id=1, source_target_pairs={{0,32},{32,64},{64,96},{96,128},{128,160},{160,192},{192,224},{1,3... | collective-permute-start | bytes 24584 | tf_op jit(solution)/shard_map/ppermute | solution.py:22
  1136.3 117.9 %collective-permute-start.49 = (bf16[16,2,128]{2,0,1:T(8,128)(2,1)S(1)}, bf16[16,2,128]{2,0,1:T(8,128)(2,1)S(1)}, u32[]{:S(2)}, u32[]{:S(2)}) collective-permute-start(bf16[16,2,128]{2,0,1:T(8,128)(2,1)S(1)} %get-tuple-element.85), channel_id=1, source_target_pairs={{32,0},{64,32},{96,64},{128,96},{160,128},{192,160},{224,192},{33,... | collective-permute-start | bytes 24584 | tf_op jit(solution)/shard_map/ppermute | solution.py:24
  1254.4 3.2 collective-permute-start.50
  1255.7 5.8 collective-permute-start.51
  1274.6 34.2 %collective-permute-start.52 = (f32[16,2,132]{2,0,1:T(8,128)S(1)}, f32[16,2,132]{2,0,1:T(8,128)S(1)}, u32[]{:S(2)}, u32[]{:S(2)}) collective-permute-start(f32[16,2,132]{2,0,1:T(8,128)S(1)} %get-tuple-element.45), channel_id=1, source_target_pairs={{0,32},{32,64},{64,96},{96,128},{128,160},{160,192},{192,224},{1,3... | collective-permute-start | bytes 50696 | tf_op jit(solution)/shard_map/ppermute | solution.py:22
  1306.9 5.2 collective-permute-start.53
  1312.3 5.7 collective-permute-start.54
  1313.6 8.5 collective-permute-start.55
  (31 other events, 578.2 us)
where the time goes:
time: 1340 us; the launch traced here: 1330 us
  blocking collectives  871 us (65%)
  starting transfers between devices  234 us (17%)
  waiting for transfers between devices  109 us (8%)
  matrix products  65.9 us (5%)
  local copies, waits for them, and re-layouts  27 us (2%)
  other arithmetic  15.5 us (1%)
    psum x4, blocking collectives, precondition(): coarse_given = lax.psum(restrict(field), 'tile')  452 us
    psum x3, blocking collectives, global_dot(): return lax.psum(products, ('band', 'tile'))  255 us
    ppermute x28, starting transfers between devices, padded_2(): lax.ppermute(tail, axis, [(i, (i + 1) % count) for i in range(ends)])  187 us
    psum x2, blocking collectives, local(): curvature = lax.psum(local_curv, ('band', 'tile'))  164 us
    ppermute x28, waiting for transfers between devices, padded_2(): lax.ppermute(head, axis, [((i + 1) % count, i) for i in range(ends)])  84.8 us
    ppermute x28, starting transfers between devices, padded_2(): lax.ppermute(head, axis, [((i + 1) % count, i) for i in range(ends)])  46.8 us
  transfers between devices with their start and end apart: 56, of which 35 were waited for; matrix products, arithmetic and copies ran while one was open for 2% of the time, Pallas kernels for 0%

commit v1 on v0

v1 whole, which is shorter than its diff:
```python
import functools

import jax
import jax.numpy as jnp
from jax import lax
from jax.experimental import pallas as pl
from jax.experimental.pallas import tpu as pltpu
from jax.sharding import PartitionSpec as P

MESH = pl.DeviceIdType.MESH
W = 2
NCB = 4
ITERS = 3
STAGES = ITERS + 1
M4 = 4
F32 = jnp.float32
BF16 = jnp.bfloat16


def loop(count, body, init=None, unroll=1):
    if init is None:

        def step(i, carry):
            body(i)
            return carry

        return lax.fori_loop(0, count, step, 0, unroll=unroll)
    return lax.fori_loop(0, count, body, init, unroll=unroll)


def dot_nn(a, b):
    return lax.dot_general(a, b, (((1,), (0,)), ((), ())), preferred_element_type=F32)


def dot_nt(a, b):
    return lax.dot_general(a, b, (((1,), (1,)), ((), ())), preferred_element_type=F32)


def halves(value):
    high = value.astype(BF16)
    low = (value - high.astype(F32)).astype(BF16)
    return jnp.concatenate([high, low], axis=0)


def kernel(
    cfg,
    tab,
    rs_hbm,
    co_hbm,
    f_hbm,
    p_hbm,
    c_hbm,
    x_out,
    r_out,
    u_out,
    rs,
    co,
    fac,
    pf,
    cf,
    pb,
    pb2,
    bmat,
    bmat2,
    zcat,
    iVO,
    iVH,
    isb,
    irb,
    VO,
    VH,
    LVO,
    LVH,
    sb,
    rb,
    UO,
    UH,
    AO,
    AH,
    FO,
    FH,
    c4O,
    c4H,
    lO,
    lH,
    lsO,
    lsH,
    TO,
    TH,
    S,
    Pp,
    y,
    ys,
    yw,
    xin,
    gin,
    run,
    prev,
    qa,
    qar,
    qb,
    qbr,
    da,
    dar,
    db,
    dbr,
    insem,
    exsem_s,
    exsem_r,
    qasem_s,
    qasem_r,
    qbsem_s,
    qbsem_r,
    dasem_s,
    dasem_r,
    dbsem_s,
    dbsem_r,
):
    n_b, n_t, nx, nz, lat, nb_blocks, kt, cols = cfg
    b = lax.axis_index("band")
    t = lax.axis_index("tile")
    z = t // nx
    x = t % nx
    own = lat
    ext = lat + 2 * W
    full = lat + 2 * M4

    loads = [
        pltpu.make_async_copy(rs_hbm, rs, insem.at[0]),
        pltpu.make_async_copy(co_hbm, co, insem.at[1]),
        pltpu.make_async_copy(p_hbm, pf, insem.at[2]),
        pltpu.make_async_copy(c_hbm, cf, insem.at[3]),
        pltpu.make_async_copy(f_hbm, fac, insem.at[4]),
    ]
    for copy in loads:
        copy.start()

    def band_at(d):
        return lax.rem(b + d + n_b, n_b)

    def tile_at(d):
        return lax.rem(t + d + n_t, n_t)

    def x_peer(d):
        return (b, z * nx + lax.rem(x + d, nx))

    def z_peer(d):
        return (b, lax.rem(t + nx * d, n_t))

    def plane_peer(d):
        return (lax.rem(b + d // nx, n_b), z * nx + lax.rem(x + lax.rem(d, nx), nx))

    n_plane = n_b * nx - 1
    barrier = pltpu.get_barrier_semaphore()

    def greet(device):
        pl.semaphore_signal(barrier, inc=1, device_id=device, device_id_type=MESH)

    loop(n_plane, lambda d: greet(plane_peer(d + 1)))
    loop(nz - 1, lambda d: greet(z_peer(d + 1)))
    for db_ in (-1, 0, 1):
        for dt_ in (-1, 1):
            greet((band_at(db_), tile_at(dt_)))
    pl.semaphore_wait(barrier, n_plane + nz - 1 + 6)

    has_n = (b > 0).astype(F32)
    has_s = (b < n_b - 1).astype(F32)
    has_w = (t > 0).astype(F32)
    has_e = (t < n_t - 1).astype(F32)

    def lane_of(rows):
        return lax.broadcasted_iota(jnp.int32, (rows, 128), 1)

    def pack_send(vO, vH, sbe, rbe, ssem, rsem):
        rows = vO.shape[1]
        lane = lane_of(rows)
        west_half = lane >= 64
        group = lane // 8
        zero = jnp.zeros((rows, 128), F32)

        def half(first_slot, first_row):
            def body(n, carry):
                tw, te = carry
                slot = first_slot + n
                row = first_row + n
                o = vO[row]
                h = vH[row]
                shift = lax.rem(8 * slot + 4, 128)
                here = group == slot
                w = pltpu.roll(jnp.where(west_half, h, o), shift, 1)
                e = pltpu.roll(jnp.where(west_half, o, h), shift, 1)
                return tw + jnp.where(here, w, 0.0), te + jnp.where(here, e, 0.0)

            return loop(ext // 2, body, (zero, zero), unroll=ext // 2)

        tw0, te0 = half(2, 0)
        tw1, te1 = half(0, ext // 2)
        for n in range(6):
            sbe[n] = vO[n]
            sbe[8 + n] = vO[ext - 6 + n]
        sbe[6] = tw0
        sbe[7] = te0
        sbe[14] = tw1
        sbe[15] = te1
        sbe[16] = te0
        sbe[17] = te1
        sbe[18] = tw0
        sbe[19] = tw1
        for first, count, to, db_, dt_ in (
            (0, 8, 8, -1, 0),
            (8, 8, 0, 1, 0),
            (16, 2, 18, 0, 1),
            (18, 2, 16, 0, -1),
            (16, 1, 22, -1, 1),
            (17, 1, 20, 1, 1),
            (18, 1, 23, -1, -1),
            (19, 1, 21, 1, -1),
        ):
            pltpu.make_async_remote_copy(
                src_ref=sbe.at[pl.ds(first, count)],
                dst_ref=rbe.at[pl.ds(to, count)],
                send_sem=ssem,
                recv_sem=rsem,
                device_id=(band_at(db_), tile_at(dt_)),
                device_id_type=MESH,
            ).start()

    def assemble(vO, sbe, rbe, rsem, emit):
        rows = vO.shape[1]
        lane = lane_of(rows)
        pltpu.make_async_copy(rbe, rbe, rsem).wait()
        low = jnp.where(lane < 48, 1.0, 0.0)
        high = jnp.where(lane >= 80, 1.0, 0.0)
        m_w = jnp.where(lane >= 124, has_w, 0.0)
        m_e = jnp.where(lane < 4, has_e, 0.0)

        def turned(slot):
            return pltpu.roll(rbe[slot], 64, 1)

        pw = (
            sbe[18] + has_w * rbe[18] + (has_n * low) * (turned(6) + has_w * turned(20)),
            sbe[19] + has_w * rbe[19] + (has_s * high) * (turned(14) + has_w * turned(22)),
        )
        pe = (
            sbe[16] + has_e * rbe[16] + (has_n * low) * (turned(7) + has_e * turned(21)),
            sbe[17] + has_e * rbe[17] + (has_s * high) * (turned(15) + has_e * turned(23)),
        )

        def finish(o, slot, half, scale, i):
            shift = lax.rem(124 - 8 * slot + 128, 128)
            w = pltpu.roll(pw[half], shift, 1)
            e = pltpu.roll(pe[half], shift, 1)
            o = jnp.where(lane < 4, w, jnp.where(lane >= 124, e, o))
            h = w * m_w + e * m_e
            if scale is not None:
                o = o * scale
                h = h * scale
            emit(i, o, h)

        for i in range(6):
            o = has_n * rbe[i]
            if i >= 2:
                o = o + vO[i - 2]
            finish(o, i, 0, has_n if i < M4 else None, i)
        mid0 = 10
        mid1 = full - 6 - 16

        def body0(n):
            finish(vO[4 + n], 6 + n, 0, None, 6 + n)

        def body1(n):
            finish(vO[14 + n], n, 1, None, 16 + n)

        loop(mid0, body0, unroll=mid0)
        loop(mid1, body1, unroll=mid1)
        for n in range(6):
            i = full - 6 + n
            o = has_s * rbe[8 + n]
            if i < full - 2:
                o = o + vO[i - 2]
            finish(o, i - 16, 1, has_s if i >= full - M4 else None, i)

    def restrict_send(k):
        def body(row, acc):
            both = halves(FO[row + W])
            part = dot_nt(both, pb[row])
            part = part[0:cols] + part[cols:] + dot_nt(both[0:cols], pb2[row])
            pick = tab[8, row]
            return tuple(acc[m] + part * (pick == m).astype(F32) for m in range(NCB))

        zero = jnp.zeros((cols, 128), F32)
        acc = loop(own, body, (zero,) * NCB, unroll=own)
        for m in range(NCB):
            qa[k, m] = acc[m]

        def send(d):
            pltpu.make_async_remote_copy(
                src_ref=qa.at[k],
                dst_ref=qar.at[k, d],
                send_sem=qasem_s.at[k],
                recv_sem=qasem_r.at[k],
                device_id=x_peer(d + 1),
                device_id_type=MESH,
            ).start()

        for d in range(nx - 1):
            send(d)

    def dots_send(k, gamma, delta, eps):
        lane = lane_of(cols)
        g = jnp.sum(gamma, axis=1, keepdims=True)
        d = jnp.sum(delta, axis=1, keepdims=True)
        e = jnp.sum(eps, axis=1, keepdims=True)
        tile = (
            jnp.where(lane == 0, g, 0.0) + jnp.where(lane == 1, d, 0.0) + jnp.where(lane == 2, e, 0.0)
        )
        da[k] = tile[0:8] + pltpu.roll(tile[8:16], 64, 1)

        def send(d):
            pltpu.make_async_remote_copy(
                src_ref=da.at[k],
                dst_ref=dar.at[k, d],
                send_sem=dasem_s.at[k],
                recv_sem=dasem_r.at[k],
                device_id=plane_peer(d + 1),
                device_id_type=MESH,
            ).start()

        loop(n_plane, send)

    def reduce_mid(k):
        pltpu.make_async_copy(qar.at[k], qar.at[k], qasem_r.at[k]).wait()
        for m in range(NCB):
            total = qa[k, m]
            for d in range(nx - 1):
                total = total + qar[k, d, m]
            qb[k, m] = total.astype(BF16)

        def send_q(d):
            pltpu.make_async_remote_copy(
                src_ref=qb.at[k],
                dst_ref=qbr.at[k, d],
                send_sem=qbsem_s.at[k],
                recv_sem=qbsem_r.at[k],
                device_id=z_peer(d + 1),
                device_id_type=MESH,
            ).start()

        for d in range(nz - 1):
            send_q(d)

    def dots_mid(k):
        pltpu.make_async_copy(dar.at[k], dar.at[k], dasem_r.at[k]).wait()
        total = da[k]
        for d in range(n_plane):
            total = total + dar[k, d]
        db[k] = total

        def send_d(d):
            pltpu.make_async_remote_copy(
                src_ref=db.at[k],
                dst_ref=dbr.at[k, d],
                send_sem=dbsem_s.at[k],
                recv_sem=dbsem_r.at[k],
                device_id=z_peer(d + 1),
                device_id_type=MESH,
            ).start()

        for d in range(nz - 1):
            send_d(d)

    def reduce_end(k):
        pltpu.make_async_copy(qbr.at[k], qbr.at[k], qbsem_r.at[k]).wait()
        for m in range(NCB):
            total = qb[k, m].astype(F32)
            for d in range(nz - 1):
                total = total + qbr[k, d, m].astype(F32)
            yw[m] = total

    def dots_end(k):
        pltpu.make_async_copy(dbr.at[k], dbr.at[k], dbsem_r.at[k]).wait()
        total = db[k]
        for d in range(nz - 1):
            total = total + dbr[k, d]
        tile = jnp.concatenate([total, pltpu.roll(total, 64, 1)], axis=0)
        shape = (cols, 128)
        return tuple(jnp.broadcast_to(tile[:, n : n + 1], shape) for n in range(3))

    def local_solve():
        lane = lane_of(cols)
        zero = jnp.zeros((cols, 128), F32)

        def flatten(j, carry):
            s = 4 * j + W
            o = pltpu.roll(FO[j], s, 1)
            h = pltpu.roll(FH[j], s, 1)
            late = lane >= s
            xin[j] = (jnp.where(late, o, h) + carry).astype(BF16)
            return jnp.where(late, h, o)

        tail = loop(ext, flatten, zero, unroll=ext)
        xin[ext] = tail.astype(BF16)

        def inner(n, acc):
            acc = acc * tab[2, n].astype(F32) + dot_nt(xin[tab[1, n]], fac[tab[0, n]])
            run[n] = acc
            return acc

        loop(nb_blocks, inner, zero, unroll=nb_blocks)

        def gather(i):
            gin[i] = run[tab[3, i]].astype(BF16)

        loop(kt, gather, unroll=kt)

        def outer(n, acc):
            acc = acc * tab[6, n].astype(F32) + dot_nn(gin[tab[5, n]], fac[tab[4, n]])
            run[n] = acc
            return acc

        loop(nb_blocks, outer, zero, unroll=nb_blocks)

        def unflatten(j, carry):
            s = 4 * j + W
            following = run[tab[7, j + 1]]
            here = pltpu.roll(carry, 128 - s, 1)
            there = pltpu.roll(following, 128 - s, 1)
            VO[j] = jnp.where(lane < 128 - s, here, there)
            VH[j] = jnp.where(lane >= 126, here, jnp.where(lane < 2, there, 0.0))
            return following

        loop(ext, unflatten, run[tab[7, 0]], unroll=ext)

    def near(value):
        lane = lane_of(cols)
        return jnp.where((lane < W) | (lane >= 128 - W), value, 0.0)

    rows24 = cols + 8
    zero24 = jnp.zeros((rows24, 128), F32)
    for row in (0, 1, ext - 2, ext - 1):
        iVO[row] = zero24
        LVO[row] = zero24[0:cols]
    iVH[...] = jnp.zeros(iVH.shape, F32)
    LVH[...] = jnp.zeros(LVH.shape, F32)
    for ref in (lO, lH, lsO, lsH, S, Pp, y, ys):
        ref[...] = jnp.zeros(ref.shape, F32)
    prev[...] = jnp.ones(prev.shape, F32)

    loads[0].wait()
    loads[1].wait()
    for row in range(own):
        value = rs[:, row, :]
        r_out[row] = value
        x_out[row] = jnp.zeros((cols, 128), F32)
        iVO[W + row, 0:cols] = value
        iVO[W + row, cols:rows24] = jnp.broadcast_to(co[row : row + 1, :], (8, 128))
    pack_send(iVO, iVH, isb, irb, exsem_s.at[0], exsem_r.at[0])

    def first_rows(row):
        FO[row + W] = r_out[row]

    loop(own, first_rows, unroll=own)
    loads[2].wait()

    def to_bf16(row):
        value = pf[row]
        high = value.astype(BF16)
        pb[row] = high
        pb2[row] = (value - high.astype(F32)).astype(BF16)

    loop(own, to_bf16, unroll=4)
    restrict_send(0)
    loads[3].wait()
    for m in range(NCB):
        value = lax.dot_general(
            cf[:, m * 128 : (m + 1) * 128],
            cf[...],
            (((0,), (0,)), ((), ())),
            precision=lax.Precision.HIGHEST,
            preferred_element_type=F32,
        )
        high = value.astype(BF16)
        bmat[m * 128 : (m + 1) * 128, :] = high
        bmat2[m * 128 : (m + 1) * 128, :] = (value - high.astype(F32)).astype(BF16)

    lane16 = lane_of(cols)

    def take_first(i, o, h):
        if isinstance(i, int):
            keep = W <= i < full - W
        else:
            keep = True
        if keep:
            FO[i - W] = o[0:cols]
            FH[i - W] = near(h[0:cols])
        inside = 0.25
        if isinstance(i, int):
            if i < M4:
                inside = 0.25 * has_n
            elif i >= full - M4:
                inside = 0.25 * has_s
        lane8 = lane16[0:8]
        side = jnp.where(lane8 >= 128 - M4, has_w, 0.0) + jnp.where(lane8 < M4, has_e, 0.0)
        c4O[i] = (o[cols:rows24] + 4.0) * inside
        c4H[i] = (h[cols:rows24] + 4.0) * (side * inside)

    assemble(iVO, isb, irb, exsem_r.at[0], take_first)
    loads[4].wait()

    side16 = jnp.where(lane16 >= 128 - M4, has_w, 0.0) + jnp.where(lane16 < M4, has_e, 0.0)
    last_lane = lane16 == 127
    first_lane = lane16 == 0

    def row_scale(i):
        north = jnp.where(i < M4, has_n, 1.0)
        south = jnp.where(i >= full - M4, has_s, 1.0)
        return 0.25 * north * south

    def apply_row(srcO, srcH, i):
        o = srcO[i]
        h = srcH[i]
        ol = pltpu.roll(o, 1, 1)
        hl = pltpu.roll(h, 1, 1)
        orr = pltpu.roll(o, 127, 1)
        hr = pltpu.roll(h, 127, 1)
        around_o = (
            srcO[i - 1]
            + srcO[i + 1]
            + jnp.where(first_lane, hl, ol)
            + jnp.where(last_lane, hr, orr)
        )
        around_h = (
            srcH[i - 1]
            + srcH[i + 1]
            + jnp.where(first_lane, ol, hl)
            + jnp.where(last_lane, orr, hr)
        )
        scale = row_scale(i)
        co_ = jnp.concatenate([c4O[i], c4O[i]], axis=0)
        ch_ = jnp.concatenate([c4H[i], c4H[i]], axis=0)
        return co_ * o - scale * around_o, ch_ * h - (scale * side16) * around_h

    def stage(k, carry):
        local_solve()
        pack_send(VO, VH, sb.at[k], rb.at[k], exsem_s.at[1 + k], exsem_r.at[1 + k])
        reduce_mid(k)

        @pl.when(k > 0)
        def _():
            dots_mid(k)

        def keep(i, o, h):
            TO[i] = o
            TH[i] = h

        assemble(VO, sb.at[k], rb.at[k], exsem_r.at[1 + k], keep)
        reduce_end(k)

        @pl.when(k > 0)
        def _():
            g, d, e = dots_end(k)
            beta = jnp.where(k > 1, g / prev[0], 0.0)
            curv = jnp.where(k > 1, d + 2.0 * beta * e + beta * beta * prev[1], d)
            alpha = g / curv
            prev[0] = g
            prev[1] = curv
            prev[2] = alpha
            prev[3] = beta

            def body(row):
                p = UO[row + M4] + beta * Pp[row]
                s = FO[row + W] + beta * S[row]
                Pp[row] = p
                S[row] = s
                x_out[row] = x_out[row] + alpha * p
                r_out[row] = r_out[row] - alpha * s

            loop(own, body, unroll=own)

        @pl.when(k == 0)
        def _():
            prev[2] = jnp.full((cols, 128), -1.0, F32)
            prev[3] = jnp.zeros((cols, 128), F32)

        alpha = prev[2]
        beta = prev[3]
        for m in range(NCB):
            ysm = yw[m] + beta * ys[m]
            ys[m] = ysm
            y[m] = y[m] - alpha * ysm

        solved = jnp.zeros((cols, NCB * 128), F32)
        for m in range(NCB):
            both = halves(y[m])
            part = dot_nn(both, bmat[m * 128 : (m + 1) * 128, :])
            solved = solved + part[0:cols] + part[cols:]
            solved = solved + dot_nn(both[0:cols], bmat2[m * 128 : (m + 1) * 128, :])
        for m in range(NCB):
            zcat[m] = halves(solved[:, m * 128 : (m + 1) * 128])

        def lift(row):
            both = zcat[tab[8, row]]
            part = dot_nn(both, pb[row])
            LVO[row + W] = part[0:cols] + part[cols:] + dot_nn(both[0:cols], pb2[row])

        loop(own, lift, unroll=own)

        @pl.when(k < STAGES - 1)
        def _():
            e = STAGES + k
            pack_send(LVO, LVH, sb.at[e], rb.at[e], exsem_s.at[1 + e], exsem_r.at[1 + e])

        def local_update(i):
            ls = TO[i] + beta * lsO[i]
            lsO[i] = ls
            lO[i] = lO[i] - alpha * ls
            ls = TH[i] + beta * lsH[i]
            lsH[i] = ls
            lH[i] = lH[i] - alpha * ls

        loop(full, local_update, unroll=8)

        @pl.when(k < STAGES - 1)
        def _():
            e = STAGES + k

            def whole(i, o, h):
                UO[i] = o + lO[i]
                UH[i] = h + lH[i]

            assemble(LVO, sb.at[e], rb.at[e], exsem_r.at[1 + e], whole)

            def once(n):
                o, h = apply_row(UO, UH, n + 1)
                AO[n + 1] = o
                AH[n + 1] = h

            loop(full - 2, once, unroll=full - 2)

            def twice(n):
                o, h = apply_row(AO, AH, n + 2)
                FO[n] = o
                FH[n] = near(h)

            loop(ext, twice, unroll=ext)

            def dots(row, acc):
                u = UO[row + M4]
                return (
                    acc[0] + u * r_out[row],
                    acc[1] + u * FO[row + W],
                    acc[2] + u * S[row],
                )

            zero = jnp.zeros((cols, 128), F32)
            dots_send(k + 1, *loop(own, dots, (zero, zero, zero), unroll=own))
            restrict_send(k + 1)

        @pl.when(k == STAGES - 1)
        def _():
            def body(row):
                u_out[row] = lO[row + M4] + LVO[row + W]

            loop(own, body, unroll=own)

        return carry

    lax.fori_loop(0, STAGES, stage, 0)

    pltpu.make_async_copy(irb, irb, exsem_s.at[0]).wait()

    def sent(e):
        pltpu.make_async_copy(rb.at[e], rb.at[e], exsem_s.at[1 + e]).wait()

    loop(2 * STAGES - 1, sent)

    def sent_q(k):
        pltpu.make_async_copy(qar.at[k], qar.at[k], qasem_s.at[k]).wait()
        pltpu.make_async_copy(qbr.at[k], qbr.at[k], qbsem_s.at[k]).wait()

    loop(STAGES, sent_q)

    def sent_d(k):
        pltpu.make_async_copy(dar.at[k + 1], dar.at[k + 1], dasem_s.at[k + 1]).wait()
        pltpu.make_async_copy(dbr.at[k + 1], dbr.at[k + 1], dbsem_s.at[k + 1]).wait()

    loop(STAGES - 1, sent_d)


def sorted_lists(keys, others, count, tiles):
    at = jnp.arange(count, dtype=jnp.int32)
    full_key = keys * 128 + at
    rank = jnp.sum((full_key[None, :] < full_key[:, None]).astype(jnp.int32), axis=1)
    place = rank[None, :] == at[:, None]

    def put(values):
        return jnp.sum(jnp.where(place, values[None, :], 0), axis=1)

    order, partner, key = put(at), put(others), put(keys)
    same = jnp.concatenate([jnp.zeros((1,), jnp.int32), (key[1:] == key[:-1]).astype(jnp.int32)])
    last = jnp.sum((keys[None, :] <= at[:, None]).astype(jnp.int32), axis=1) - 1
    return [order, partner, same, last]


def local(n_b, n_t, right_side, coeff_field, factor_blocks, block_rows, block_cols, prolong, coarse_picks, coarse_factor):
    cols, lat, lon = right_side.shape
    count = factor_blocks.shape[2]
    ext = lat + 2 * W
    full = lat + 2 * M4
    kt = (ext * (lon + 2 * W) + 127) // 128
    nx = 4 if n_t % 4 == 0 and n_t > 4 else 2
    nz = n_t // nx
    rows_idx = block_rows[0, 0]
    cols_idx = block_cols[0, 0]
    picks = jnp.pad(coarse_picks[:, 0, 0], (0, count - lat))
    tab = jnp.stack(
        sorted_lists(rows_idx, cols_idx, count, kt) + sorted_lists(cols_idx, rows_idx, count, kt) + [picks]
    )
    cfg = (n_b, n_t, nx, nz, lat, count, kt, cols)
    n_plane = n_b * nx - 1
    rows24 = cols + 8
    vm = pltpu.VMEM
    ext_f = vm((ext, cols, 128), F32)
    full_f = vm((full, cols, 128), F32)
    own_f = vm((lat, cols, 128), F32)
    n_ex = 2 * STAGES - 1
    dma = pltpu.SemaphoreType.DMA
    scratch = [
        vm((cols, lat, lon), F32),
        vm((lat, lon), F32),
        vm((count, 128, 128), BF16),
        vm((lat, 128, 128), F32),
        vm(coarse_factor.shape[1:], F32),
        vm((lat, 128, 128), BF16),
        vm((lat, 128, 128), BF16),
        vm(coarse_factor.shape[1:], BF16),
        vm(coarse_factor.shape[1:], BF16),
        vm((NCB, 2 * cols, 128), BF16),
        vm((ext, rows24, 128), F32),
        vm((ext, rows24, 128), F32),
        vm((24, rows24, 128), F32),
        vm((24, rows24, 128), F32),
        ext_f,
        ext_f,
        ext_f,
        ext_f,
        vm((n_ex, 24, cols, 128), F32),
        vm((n_ex, 24, cols, 128), F32),
        full_f,
        full_f,
        full_f,
        full_f,
        ext_f,
        ext_f,
        vm((full, 8, 128), F32),
        vm((full, 8, 128), F32),
        full_f,
        full_f,
        full_f,
        full_f,
        full_f,
        full_f,
        own_f,
        own_f,
        vm((NCB, cols, 128), F32),
        vm((NCB, cols, 128), F32),
        vm((NCB, cols, 128), F32),
        vm((kt, cols, 128), BF16),
        vm((kt, cols, 128), BF16),
        vm((count, cols, 128), F32),
        vm((4, cols, 128), F32),
        vm((STAGES, NCB, cols, 128), F32),
        vm((STAGES, nx - 1, NCB, cols, 128), F32),
        vm((STAGES, NCB, cols, 128), BF16),
        vm((STAGES, nz - 1, NCB, cols, 128), BF16),
        vm((STAGES, 8, 128), F32),
        vm((STAGES, n_plane, 8, 128), F32),
        vm((STAGES, 8, 128), F32),
        vm((STAGES, nz - 1, 8, 128), F32),
        dma((5,)),
        dma((1 + n_ex,)),
        dma((1 + n_ex,)),
    ] + [dma((STAGES,))] * 8
    any_spec = pl.BlockSpec(memory_space=pl.ANY)
    out = jax.ShapeDtypeStruct((lat, cols, 128), F32)
    outs = pl.pallas_call(
        functools.partial(kernel, cfg),
        out_shape=(out, out, out),
        in_specs=[pl.BlockSpec(memory_space=pltpu.SMEM)] + [any_spec] * 5,
        out_specs=(pl.BlockSpec(memory_space=pltpu.VMEM),) * 3,
        scratch_shapes=scratch,
        compiler_params=pltpu.CompilerParams(
            collective_id=3, has_side_effects=True, vmem_limit_bytes=48 << 20
        ),
    )(
        tab,
        right_side,
        coeff_field,
        factor_blocks.reshape(factor_blocks.shape[2:]),
        prolong.reshape(lat, 128, lon),
        coarse_factor.reshape(coarse_factor.shape[1:]),
    )
    return tuple(jnp.transpose(value, (1, 0, 2)) for value in outs)


def solution(mesh):
    in_specs = (
        P(None, "band", "tile"),
        P("band", "tile"),
        P("band", "tile", None, None, None),
        P("band", "tile", None),
        P("band", "tile", None),
        P("band", None, None, "tile"),
        P("band", "tile", None),
        P("band", None, None),
    )
    out_specs = (P(None, "band", "tile"),) * 3
    return jax.shard_map(
        functools.partial(local, mesh.shape["band"], mesh.shape["tile"]),
        mesh=mesh,
        in_specs=in_specs,
        out_specs=out_specs,
        check_vma=False,
    )
```

time: 1340 us -> 97.2 us (0.07); the launches traced: 1330 us -> 96.9 us
  blocking collectives: 871 us -> 0 us
  starting transfers between devices: 234 us -> 0 us
  waiting for transfers between devices: 109 us -> 0 us
  Pallas kernels: 0 us -> 86.2 us
  matrix products: 65.9 us -> 0 us
  local copies, waits for them, and re-layouts: 27 us -> 7.18 us
    psum x9 -> x0, blocking collectives: 871 us -> none  [the longest x4 452 us: precondition(): coarse_given = lax.psum(restrict(field), 'tile')]
    ppermute x56 -> x0, starting transfers between devices: 234 us -> none  [the longest x28 187 us: padded_2(): lax.ppermute(tail, axis, [(i, (i + 1) % count) for i in range(ends)])]
    ppermute x56 -> x0, waiting for transfers between devices: 109 us -> none  [the longest x28 84.8 us: padded_2(): lax.ppermute(head, axis, [((i + 1) % count, i) for i in range(ends)])]
    pallas_call x0 -> x1, Pallas kernels: none -> 86.2 us  [local(): pl.pallas_call(functools.partial(kernel, cfg), out_shape=(out, out, out),...]
    dot_general x40 -> x0, matrix products: 65.9 us -> none  [the longest x4 16.9 us: block_solve(): jnp.einsum('bij,bcj->bci', factor, pieces[cols_idx], preferred_element_ty...]
  transfers between devices with their start and end apart: 56 -> 0, of which waited for: 35 -> 0; matrix products, arithmetic and copies ran while one was open for 2% -> 0% of each run, Pallas kernels for 0% -> 0%
where the time goes in v1:
time: 97.2 us; the launch traced here: 96.9 us
  Pallas kernels  86.2 us (89%)
  local copies, waits for them, and re-layouts  7.18 us (7%)
  other arithmetic  2.85 us (3%)
    pallas_call x1, Pallas kernels, local(): pl.pallas_call(functools.partial(kernel, cfg), out_shape=(out, out, out),...  86.2 us
    unnamed x11, local copies, waits for them, and re-layouts  6.48 us

profile of v1, /device:TPU:1, one launch (start us, length us, event | category | flops | bytes accessed | tf_op | source)
XLA Modules:
  0.0 96.9 jit_solution(1758732797398371857)
XLA Ops:
  0.6 0.7 pad_bitcast_fusion
  1.3 0.7 iota_add_fusion.1
  1.9 0.2 convert_reduce_fusion.3
  2.1 0.7 iota_add_fusion
  2.8 0.2 convert_reduce_fusion.1
  3.0 0.9 convert_reduce_fusion
  3.9 0.1 slice_compare_fusion
  4.0 0.1 fusion.2
  4.1 0.1 fusion.3
  4.2 0.0 copy-start
  4.2 1.4 %copy-done = f32[24,1,128,128]{3,2,1,0:T(8,128)S(1)} copy-done((f32[24,1,128,128]{3,2,1,0:T(8,128)S(1)}, f32[24,1,128,128]{3,2,1,0:T(8,128)}, u32[]{:S(2)}) %copy-start) | copy-done | bytes 1572888
  5.6 0.0 copy-start.1
  5.6 1.2 %copy-done.1 = f32[1,512,512]{2,1,0:T(8,128)S(1)} copy-done((f32[1,512,512]{2,1,0:T(8,128)S(1)}, f32[1,512,512]{2,1,0:T(8,128)}, u32[]{:S(2)}) %copy-start.1) | copy-done | bytes 1048600
  6.8 0.0 copy-start.2
  6.8 0.9 copy-done.2
  7.8 0.0 copy-start.3
  7.8 0.7 copy-done.3
  8.5 86.2 %shard_map.103 = (f32[24,16,128]{2,1,0:T(8,128)S(1)}, f32[24,16,128]{2,1,0:T(8,128)S(1)}, f32[24,16,128]{2,1,0:T(8,128)S(1)}) custom-call(s32[9,116]{1,0:T(8,128)S(1)} %stack.41.tab, f32[16,24,128]{2,1,0:T(8,128)S(1)} %copy-done.2, f32[24,128]{1,0:T(8,128)S(1)} %copy-done.3, bf16[116,128,128]{2,1,0:T(8,128)(2,1)} %bitcast.30, f32[24,128,128]{2,1,0:T(8,128)S(1)} %bitcast.25, ...), custom_call_target="tpu_custom_call" | custom-call | tf_op jit(solution)/shard_map/pallas_call | solution.py:786
  94.7 0.7 copy.14
  95.5 0.7 copy.15
  96.2 0.7 copy.16
  (2 shorter events, 0.0 us)
Async XLA Ops:
  4.2 1.4 %copy-start = (f32[24,1,128,128]{3,2,1,0:T(8,128)S(1)}, f32[24,1,128,128]{3,2,1,0:T(8,128)}, u32[]{:S(2)}) copy-start(f32[24,1,128,128]{3,2,1,0:T(8,128)} %param.13) | copy-start | bytes 4718596
  5.6 1.2 %copy-start.1 = (f32[1,512,512]{2,1,0:T(8,128)S(1)}, f32[1,512,512]{2,1,0:T(8,128)}, u32[]{:S(2)}) copy-start(f32[1,512,512]{2,1,0:T(8,128)} %param.15) | copy-start | bytes 3145732
  6.8 0.9 copy-start.2
  7.8 0.7 copy-start.3

commit v2 on v1

--- a/solution.py
+++ b/solution.py
@@ -42,80 +42,26 @@
     return jnp.concatenate([high, low], axis=0)
 
 
-def kernel(
-    cfg,
-    tab,
-    rs_hbm,
-    co_hbm,
-    f_hbm,
-    p_hbm,
-    c_hbm,
-    x_out,
-    r_out,
-    u_out,
-    rs,
-    co,
-    fac,
-    pf,
-    cf,
-    pb,
-    pb2,
-    bmat,
-    bmat2,
-    zcat,
-    iVO,
-    iVH,
-    isb,
-    irb,
-    VO,
-    VH,
-    LVO,
-    LVH,
-    sb,
-    rb,
-    UO,
-    UH,
-    AO,
-    AH,
-    FO,
-    FH,
-    c4O,
-    c4H,
-    lO,
-    lH,
-    lsO,
-    lsH,
-    TO,
-    TH,
-    S,
-    Pp,
-    y,
-    ys,
-    yw,
-    xin,
-    gin,
-    run,
-    prev,
-    qa,
-    qar,
-    qb,
-    qbr,
-    da,
-    dar,
-    db,
-    dbr,
-    insem,
-    exsem_s,
-    exsem_r,
-    qasem_s,
-    qasem_r,
-    qbsem_s,
-    qbsem_r,
-    dasem_s,
-    dasem_r,
-    dbsem_s,
-    dbsem_r,
-):
+def kernel(cfg, names, *refs):
+    r = dict(zip(names, refs))
+    rs_hbm, co_hbm, f_hbm, p_hbm, c_hbm = (r[n] for n in ("rs_hbm", "co_hbm", "f_hbm", "p_hbm", "c_hbm"))
+    x_out, r_out = r["xst"], r["rst"]
+    picks, tab, tabv, lists = r["picks"], r["tab"], r["tabv"], r["lists"]
+    rs, co, fac, pf, cf = r["rs"], r["co"], r["fac"], r["pf"], r["cf"]
+    pb, pb2, bmat, bmat2, zcat = r["pb"], r["pb2"], r["bmat"], r["bmat2"], r["zcat"]
+    iVO, iVH, isb, irb = r["iVO"], r["iVH"], r["isb"], r["irb"]
+    VO, VH, sb, rb = r["VO"], r["VH"], r["sb"], r["rb"]
+    LV, pk, nsb, nrb = r["LV"], r["pk"], r["nsb"], r["nrb"]
+    pht, phr, ph, ph2, pm = r["pht"], r["phr"], r["ph"], r["ph2"], r["pm"]
+    UO, UH, AO, AH, FO, FH = r["UO"], r["UH"], r["AO"], r["AH"], r["FO"], r["FH"]
+    c4O, c4H, MsO, MsH, TO, TH = r["c4O"], r["c4H"], r["MsO"], r["MsH"], r["TO"], r["TH"]
+    S, Pp, yw, xin, gin, run, prev = r["S"], r["Pp"], r["yw"], r["xin"], r["gin"], r["run"], r["prev"]
+    qa, qar, qb, qbr = r["qa"], r["qar"], r["qb"], r["qbr"]
+    da, dar, db, dbr = r["da"], r["dar"], r["db"], r["dbr"]
+    insem, exsem_s, exsem_r = r["insem"], r["exsem_s"], r["exsem_r"]
+    nssem_s, nssem_r, phsem_s, phsem_r = r["nssem_s"], r["nssem_r"], r["phsem_s"], r["phsem_r"]
+    qasem_s, qasem_r, qbsem_s, qbsem_r = r["qasem_s"], r["qasem_r"], r["qbsem_s"], r["qbsem_r"]
+    dasem_s, dasem_r, dbsem_s, dbsem_r = r["dasem_s"], r["dasem_r"], r["dbsem_s"], r["dbsem_r"]
     n_b, n_t, nx, nz, lat, nb_blocks, kt, cols = cfg
     b = lax.axis_index("band")
     t = lax.axis_index("tile")
@@ -125,13 +71,9 @@
     ext = lat + 2 * W
     full = lat + 2 * M4
 
-    loads = [
-        pltpu.make_async_copy(rs_hbm, rs, insem.at[0]),
-        pltpu.make_async_copy(co_hbm, co, insem.at[1]),
-        pltpu.make_async_copy(p_hbm, pf, insem.at[2]),
-        pltpu.make_async_copy(c_hbm, cf, insem.at[3]),
-        pltpu.make_async_copy(f_hbm, fac, insem.at[4]),
-    ]
+    sources = (r["br_hbm"], r["bc_hbm"], rs_hbm, co_hbm, p_hbm, c_hbm, f_hbm)
+    targets = (r["br"], r["bc"], rs, co, pf, cf, fac)
+    loads = [pltpu.make_async_copy(a, c, insem.at[n]) for n, (a, c) in enumerate(zip(sources, targets))]
     for copy in loads:
         copy.start()
 
@@ -161,7 +103,6 @@
     for db_ in (-1, 0, 1):
         for dt_ in (-1, 1):
             greet((band_at(db_), tile_at(dt_)))
-    pl.semaphore_wait(barrier, n_plane + nz - 1 + 6)
 
     has_n = (b > 0).astype(F32)
     has_s = (b < n_b - 1).astype(F32)
@@ -171,7 +112,7 @@
     def lane_of(rows):
         return lax.broadcasted_iota(jnp.int32, (rows, 128), 1)
 
-    def pack_send(vO, vH, sbe, rbe, ssem, rsem):
+    def pack(vO, vH, sbe):
         rows = vO.shape[1]
         lane = lane_of(rows)
         west_half = lane >= 64
@@ -206,6 +147,8 @@
         sbe[17] = te1
         sbe[18] = tw0
         sbe[19] = tw1
+
+    def send_eight(sbe, rbe, ssem, rsem):
         for first, count, to, db_, dt_ in (
             (0, 8, 8, -1, 0),
             (8, 8, 0, 1, 0),
@@ -280,20 +223,19 @@
                 o = o + vO[i - 2]
             finish(o, i - 16, 1, has_s if i >= full - M4 else None, i)
 
-    def restrict_send(k):
-        def body(row, acc):
+    def restrict(first, count, acc):
+        def body(n, acc):
+            row = first + n
             both = halves(FO[row + W])
             part = dot_nt(both, pb[row])
             part = part[0:cols] + part[cols:] + dot_nt(both[0:cols], pb2[row])
-            pick = tab[8, row]
+            pick = picks[row]
             return tuple(acc[m] + part * (pick == m).astype(F32) for m in range(NCB))
 
-        zero = jnp.zeros((cols, 128), F32)
-        acc = loop(own, body, (zero,) * NCB, unroll=own)
-        for m in range(NCB):
-            qa[k, m] = acc[m]
-
-        def send(d):
+        return loop(count, body, acc, unroll=count)
+
+    def send_x(k):
+        for d in range(nx - 1):
             pltpu.make_async_remote_copy(
                 src_ref=qa.at[k],
                 dst_ref=qar.at[k, d],
@@ -302,9 +244,6 @@
                 device_id=x_peer(d + 1),
                 device_id_type=MESH,
             ).start()
-
-        for d in range(nx - 1):
-            send(d)
 
     def dots_send(k, gamma, delta, eps):
         lane = lane_of(cols)
@@ -435,32 +374,68 @@
         lane = lane_of(cols)
         return jnp.where((lane < W) | (lane >= 128 - W), value, 0.0)
 
+    def spread_out(row):
+        return jnp.broadcast_to(row, (128, 128))
+
+    lane128 = lane_of(128)
+    sub128 = lax.broadcasted_iota(jnp.int32, (128, 128), 0)
+
+    def sort_list(first, keys, others):
+        keys_sub = jnp.transpose(spread_out(keys))
+        others_sub = jnp.transpose(spread_out(others))
+        key_lane = spread_out(keys) * 128 + lane128
+        key_sub = keys_sub * 128 + sub128
+        rank = jnp.sum((key_lane < key_sub).astype(jnp.int32), axis=1, keepdims=True)
+        place = rank == lane128
+
+        def put(values):
+            return jnp.sum(jnp.where(place, values, 0), axis=0, keepdims=True)
+
+        ordered = put(keys_sub)
+        before = pltpu.roll(ordered, 1, 1)
+        same = jnp.where((ordered == before) & (lane128[0:1] > 0), 1, 0)
+        tabv[first : first + 1, :] = put(sub128)
+        tabv[first + 1 : first + 2, :] = put(others_sub)
+        tabv[first + 2 : first + 3, :] = same
+        tabv[first + 3 : first + 4, :] = (
+            jnp.sum((keys_sub <= lane128).astype(jnp.int32), axis=0, keepdims=True) - 1
+        )
+
+    lists[...] = jnp.full(lists.shape, 100, jnp.int32)
+    loads[0].wait()
+    loads[1].wait()
+    lists[0:1, 0:nb_blocks] = r["br"][0]
+    lists[1:2, 0:nb_blocks] = r["bc"][0]
+    sort_list(0, lists[0:1, :], lists[1:2, :])
+    sort_list(4, lists[1:2, :], lists[0:1, :])
+    to_smem = pltpu.make_async_copy(tabv, tab, insem.at[7])
+    to_smem.start()
+
     rows24 = cols + 8
     zero24 = jnp.zeros((rows24, 128), F32)
+    zero = jnp.zeros((cols, 128), F32)
+    lane16 = lane_of(cols)
     for row in (0, 1, ext - 2, ext - 1):
         iVO[row] = zero24
-        LVO[row] = zero24[0:cols]
     iVH[...] = jnp.zeros(iVH.shape, F32)
-    LVH[...] = jnp.zeros(LVH.shape, F32)
-    for ref in (lO, lH, lsO, lsH, S, Pp, y, ys):
+    for ref in (UO, UH, MsO, MsH, S, Pp):
         ref[...] = jnp.zeros(ref.shape, F32)
     prev[...] = jnp.ones(prev.shape, F32)
-
-    loads[0].wait()
-    loads[1].wait()
+    prev[2] = jnp.full((cols, 128), -1.0, F32)
+    prev[3] = zero
+
+    loads[2].wait()
+    loads[3].wait()
     for row in range(own):
         value = rs[:, row, :]
         r_out[row] = value
-        x_out[row] = jnp.zeros((cols, 128), F32)
+        FO[row + W] = value
+        x_out[row] = zero
         iVO[W + row, 0:cols] = value
         iVO[W + row, cols:rows24] = jnp.broadcast_to(co[row : row + 1, :], (8, 128))
-    pack_send(iVO, iVH, isb, irb, exsem_s.at[0], exsem_r.at[0])
-
-    def first_rows(row):
-        FO[row + W] = r_out[row]
-
-    loop(own, first_rows, unroll=own)
-    loads[2].wait()
+    pack(iVO, iVH, isb)
+
+    loads[4].wait()
 
     def to_bf16(row):
         value = pf[row]
@@ -469,8 +444,44 @@
         pb2[row] = (value - high.astype(F32)).astype(BF16)
 
     loop(own, to_bf16, unroll=4)
-    restrict_send(0)
-    loads[3].wait()
+    acc = restrict(0, own, (zero,) * NCB)
+    for m in range(NCB):
+        qa[0, m] = acc[m]
+
+    group128 = lane128 // 8
+    group8 = group128[0:8]
+    sub8 = sub128[0:8]
+    for half, first_slot, first_row in ((0, M4, 0), (1, 0, 16 - M4)):
+
+        def columns(n, carry):
+            slot = first_slot + n
+            turned = pltpu.roll(pf[first_row + n], lax.rem(8 * slot + 4, 128), 1)
+            chosen = (group8 == slot) & (sub8 == picks[first_row + n])
+            return (
+                carry[0] + jnp.where(group128 == slot, turned, 0.0),
+                carry[1] + jnp.where(chosen, 1.0, 0.0),
+            )
+
+        values, masks = loop(
+            own // 2, columns, (jnp.zeros((128, 128), F32), jnp.zeros((8, 128), F32)), unroll=4
+        )
+        pht[half, 0:128] = values
+        pht[half, 128:136] = masks
+
+    pl.semaphore_wait(barrier, n_plane + nz - 1 + 6)
+    send_eight(isb, irb, exsem_s.at[0], exsem_r.at[0])
+    send_x(0)
+    for n, d in enumerate((1, -1)):
+        pltpu.make_async_remote_copy(
+            src_ref=pht,
+            dst_ref=phr.at[n],
+            send_sem=phsem_s.at[n],
+            recv_sem=phsem_r.at[n],
+            device_id=(b, tile_at(d)),
+            device_id_type=MESH,
+        ).start()
+
+    loads[5].wait()
     for m in range(NCB):
         value = lax.dot_general(
             cf[:, m * 128 : (m + 1) * 128],
@@ -482,8 +493,6 @@
         high = value.astype(BF16)
         bmat[m * 128 : (m + 1) * 128, :] = high
         bmat2[m * 128 : (m + 1) * 128, :] = (value - high.astype(F32)).astype(BF16)
-
-    lane16 = lane_of(cols)
 
     def take_first(i, o, h):
         if isinstance(i, int):
@@ -505,7 +514,8 @@
         c4H[i] = (h[cols:rows24] + 4.0) * (side * inside)
 
     assemble(iVO, isb, irb, exsem_r.at[0], take_first)
-    loads[4].wait()
+    loads[6].wait()
+    to_smem.wait()
 
     side16 = jnp.where(lane16 >= 128 - M4, has_w, 0.0) + jnp.where(lane16 < M4, has_e, 0.0)
     last_lane = lane16 == 127
@@ -540,21 +550,91 @@
         ch_ = jnp.concatenate([c4H[i], c4H[i]], axis=0)
         return co_ * o - scale * around_o, ch_ * h - (scale * side16) * around_h
 
+    def once(i):
+        o, h = apply_row(UO, UH, i)
+        AO[i] = o
+        AH[i] = h
+
+    def twice(i):
+        o, h = apply_row(AO, AH, i)
+        FO[i - W] = o
+        FH[i - W] = near(h)
+
+    def lift(first, count):
+        def body(n):
+            row = first + n
+            both = zcat[picks[row]]
+            part = dot_nn(both, pb[row])
+            LV[row] = part[0:cols] + part[cols:] + dot_nn(both[0:cols], pb2[row])
+
+        loop(count, body, unroll=count)
+
     def stage(k, carry):
         local_solve()
-        pack_send(VO, VH, sb.at[k], rb.at[k], exsem_s.at[1 + k], exsem_r.at[1 + k])
         reduce_mid(k)
+        pack(VO, VH, sb.at[k])
+        send_eight(sb.at[k], rb.at[k], exsem_s.at[1 + k], exsem_r.at[1 + k])
 
         @pl.when(k > 0)
         def _():
             dots_mid(k)
 
+        @pl.when(k == 0)
+        def _():
+            for n in range(2):
+                pltpu.make_async_copy(phr.at[n], phr.at[n], phsem_r.at[n]).wait()
+            from_west = lax.rem(lane128, 8) < M4
+            for half in range(2):
+                value = jnp.where(from_west, has_w * phr[0, half, 0:128], has_e * phr[1, half, 0:128])
+                high = value.astype(BF16)
+                ph[half] = high
+                ph2[half] = (value - high.astype(F32)).astype(BF16)
+                pm[half] = jnp.where(from_west[0:8], phr[0, half, 128:136], phr[1, half, 128:136])
+
         def keep(i, o, h):
             TO[i] = o
             TH[i] = h
 
         assemble(VO, sb.at[k], rb.at[k], exsem_r.at[1 + k], keep)
         reduce_end(k)
+
+        solved = jnp.zeros((cols, NCB * 128), F32)
+        for m in range(NCB):
+            both = halves(yw[m])
+            part = dot_nn(both, bmat[m * 128 : (m + 1) * 128, :])
+            solved = solved + part[0:cols] + part[cols:]
+            solved = solved + dot_nn(both[0:cols], bmat2[m * 128 : (m + 1) * 128, :])
+        for m in range(NCB):
+            zcat[m] = halves(solved[:, m * 128 : (m + 1) * 128])
+        lift(0, M4)
+        lift(own - M4, M4)
+        for half in range(2):
+            total = zero
+            for m in range(NCB):
+                both = zcat[m]
+                part = dot_nn(both, ph[half])
+                part = part[0:cols] + part[cols:] + dot_nn(both[0:cols], ph2[half])
+                total = total + part * jnp.broadcast_to(pm[half, m : m + 1, :], (cols, 128))
+            pk[half] = total
+
+        @pl.when(k < STAGES - 1)
+        def _():
+            for n in range(M4):
+                nsb[k, n] = LV[n]
+                nsb[k, M4 + 1 + n] = LV[own - M4 + n]
+            nsb[k, M4] = pk[0]
+            nsb[k, 2 * M4 + 1] = pk[1]
+            for first, to, d in ((0, M4 + 1, -1), (M4 + 1, 0, 1)):
+                pltpu.make_async_remote_copy(
+                    src_ref=nsb.at[k, pl.ds(first, M4 + 1)],
+                    dst_ref=nrb.at[k, pl.ds(to, M4 + 1)],
+                    send_sem=nssem_s.at[k],
+                    recv_sem=nssem_r.at[k],
+                    device_id=(band_at(d), t),
+                    device_id_type=MESH,
+                ).start()
+
+        lift(M4, own - 2 * M4)
 
         @pl.when(k > 0)
         def _():
@@ -577,72 +657,52 @@
 
             loop(own, body, unroll=own)
 
-        @pl.when(k == 0)
-        def _():
-            prev[2] = jnp.full((cols, 128), -1.0, F32)
-            prev[3] = jnp.zeros((cols, 128), F32)
-
         alpha = prev[2]
         beta = prev[3]
-        for m in range(NCB):
-            ysm = yw[m] + beta * ys[m]
-            ys[m] = ysm
-            y[m] = y[m] - alpha * ysm
-
-        solved = jnp.zeros((cols, NCB * 128), F32)
-        for m in range(NCB):
-            both = halves(y[m])
-            part = dot_nn(both, bmat[m * 128 : (m + 1) * 128, :])
-            solved = solved + part[0:cols] + part[cols:]
-            solved = solved + dot_nn(both[0:cols], bmat2[m * 128 : (m + 1) * 128, :])
-        for m in range(NCB):
-            zcat[m] = halves(solved[:, m * 128 : (m + 1) * 128])
-
-        def lift(row):
-            both = zcat[tab[8, row]]
-            part = dot_nn(both, pb[row])
-            LVO[row + W] = part[0:cols] + part[cols:] + dot_nn(both[0:cols], pb2[row])
-
-        loop(own, lift, unroll=own)
+
+        def combine(i, o, h):
+            ms = TO[i] + o + beta * MsO[i]
+            MsO[i] = ms
+            UO[i] = UO[i] - alpha * ms
+            ms = TH[i] + h + beta * MsH[i]
+            MsH[i] = ms
+            UH[i] = UH[i] - alpha * ms
+
+        for half, first_slot, first_row in ((0, M4, 0), (1, 0, 16 - M4)):
+            strip = pk[half]
+
+            def inner_rows(n):
+                slot = first_slot + n
+                h = pltpu.roll(strip, lax.rem(252 - 8 * slot, 128), 1) * side16
+                combine(16 * half + slot, LV[first_row + n], h)
+
+            loop(own // 2, inner_rows, unroll=own // 2)
 
         @pl.when(k < STAGES - 1)
         def _():
-            e = STAGES + k
-            pack_send(LVO, LVH, sb.at[e], rb.at[e], exsem_s.at[1 + e], exsem_r.at[1 + e])
-
-        def local_update(i):
-            ls = TO[i] + beta * lsO[i]
-            lsO[i] = ls
-            lO[i] = lO[i] - alpha * ls
-            ls = TH[i] + beta * lsH[i]
-            lsH[i] = ls
-            lH[i] = lH[i] - alpha * ls
-
-        loop(full, local_update, unroll=8)
-
-        @pl.when(k < STAGES - 1)
-        def _():
-            e = STAGES + k
-
-            def whole(i, o, h):
-                UO[i] = o + lO[i]
-                UH[i] = h + lH[i]
-
-            assemble(LVO, sb.at[e], rb.at[e], exsem_r.at[1 + e], whole)
-
-            def once(n):
-                o, h = apply_row(UO, UH, n + 1)
-                AO[n + 1] = o
-                AH[n + 1] = h
-
-            loop(full - 2, once, unroll=full - 2)
-
-            def twice(n):
-                o, h = apply_row(AO, AH, n + 2)
-                FO[n] = o
-                FH[n] = near(h)
-
-            loop(ext, twice, unroll=ext)
+            loop(full - 10, lambda n: once(5 + n), unroll=full - 10)
+            loop(full - 12, lambda n: twice(6 + n), unroll=full - 12)
+            acc = restrict(2, own - 4, (zero,) * NCB)
+
+            pltpu.make_async_copy(nrb.at[k], nrb.at[k], nssem_r.at[k]).wait()
+            for n in range(M4):
+                combine(n, nrb[k, n] * has_n, pltpu.roll(nrb[k, M4], 60 - 8 * n, 1) * (has_n * side16))
+                combine(
+                    full - M4 + n,
+                    nrb[k, M4 + 1 + n] * has_s,
+                    pltpu.roll(nrb[k, 2 * M4 + 1], 92 - 8 * n, 1) * (has_s * side16),
+                )
+            for n in range(4):
+                once(1 + n)
+                once(full - 5 + n)
+            for n in range(4):
+                twice(2 + n)
+                twice(full - 6 + n)
+            acc = restrict(0, 2, acc)
+            acc = restrict(own - 2, 2, acc)
+            for m in range(NCB):
+                qa[k + 1, m] = acc[m]
+            send_x(k + 1)
 
             def dots(row, acc):
                 u = UO[row + M4]
@@ -652,14 +712,14 @@
                     acc[2] + u * S[row],
                 )
 
-            zero = jnp.zeros((cols, 128), F32)
             dots_send(k + 1, *loop(own, dots, (zero, zero, zero), unroll=own))
-            restrict_send(k + 1)
 
         @pl.when(k == STAGES - 1)
         def _():
             def body(row):
-                u_out[row] = lO[row + M4] + LVO[row + W]
+                r["x_out"][:, row, :] = x_out[row]
+                r["r_out"][:, row, :] = r_out[row]
+                r["u_out"][:, row, :] = UO[row + M4]
 
             loop(own, body, unroll=own)
 
@@ -672,7 +732,14 @@
     def sent(e):
         pltpu.make_async_copy(rb.at[e], rb.at[e], exsem_s.at[1 + e]).wait()
 
-    loop(2 * STAGES - 1, sent)
+    loop(STAGES, sent)
+    for n in range(2):
+        pltpu.make_async_copy(phr.at[n], phr.at[n], phsem_s.at[n]).wait()
+
+    def sent_ns(k):
+        pltpu.make_async_copy(nrb.at[k], nrb.at[k], nssem_s.at[k]).wait()
+
+    loop(STAGES - 1, sent_ns)
 
     def sent_q(k):
         pltpu.make_async_copy(qar.at[k], qar.at[k], qasem_s.at[k]).wait()
@@ -685,21 +752,6 @@
         pltpu.make_async_copy(dbr.at[k + 1], dbr.at[k + 1], dbsem_s.at[k + 1]).wait()
 
     loop(STAGES - 1, sent_d)
-
-
-def sorted_lists(keys, others, count, tiles):
-    at = jnp.arange(count, dtype=jnp.int32)
-    full_key = keys * 128 + at
-    rank = jnp.sum((full_key[None, :] < full_key[:, None]).astype(jnp.int32), axis=1)
-    place = rank[None, :] == at[:, None]
-
-    def put(values):
-        return jnp.sum(jnp.where(place, values[None, :], 0), axis=1)
-
-    order, partner, key = put(at), put(others), put(keys)
-    same = jnp.concatenate([jnp.zeros((1,), jnp.int32), (key[1:] == key[:-1]).astype(jnp.int32)])
-    last = jnp.sum((keys[None, :] <= at[:, None]).astype(jnp.int32), axis=1) - 1
-    return [order, partner, same, last]
 
 
 def local(n_b, n_t, right_side, coeff_field, factor_blocks, block_rows, block_cols, prolong, coarse_picks, coarse_factor):
@@ -710,12 +762,6 @@
     kt = (ext * (lon + 2 * W) + 127) // 128
     nx = 4 if n_t % 4 == 0 and n_t > 4 else 2
     nz = n_t // nx
-    rows_idx = block_rows[0, 0]
-    cols_idx = block_cols[0, 0]
-    picks = jnp.pad(coarse_picks[:, 0, 0], (0, count - lat))
-    tab = jnp.stack(
-        sorted_lists(rows_idx, cols_idx, count, kt) + sorted_lists(cols_idx, rows_idx, count, kt) + [picks]
-    )
     cfg = (n_b, n_t, nx, nz, lat, count, kt, cols)
     n_plane = n_b * nx - 1
     rows24 = cols + 8
@@ -723,84 +769,113 @@
     ext_f = vm((ext, cols, 128), F32)
     full_f = vm((full, cols, 128), F32)
     own_f = vm((lat, cols, 128), F32)
-    n_ex = 2 * STAGES - 1
+    cn = coarse_factor.shape[1:]
+    four = vm((NCB, cols, 128), F32)
     dma = pltpu.SemaphoreType.DMA
-    scratch = [
-        vm((cols, lat, lon), F32),
-        vm((lat, lon), F32),
-        vm((count, 128, 128), BF16),
-        vm((lat, 128, 128), F32),
-        vm(coarse_factor.shape[1:], F32),
-        vm((lat, 128, 128), BF16),
-        vm((lat, 128, 128), BF16),
-        vm(coarse_factor.shape[1:], BF16),
-        vm(coarse_factor.shape[1:], BF16),
-        vm((NCB, 2 * cols, 128), BF16),
-        vm((ext, rows24, 128), F32),
-        vm((ext, rows24, 128), F32),
-        vm((24, rows24, 128), F32),
-        vm((24, rows24, 128), F32),
-        ext_f,
-        ext_f,
-        ext_f,
-        ext_f,
-        vm((n_ex, 24, cols, 128), F32),
-        vm((n_ex, 24, cols, 128), F32),
-        full_f,
-        full_f,
-        full_f,
-        full_f,
-        ext_f,
-        ext_f,
-        vm((full, 8, 128), F32),
-        vm((full, 8, 128), F32),
-        full_f,
-        full_f,
-        full_f,
-        full_f,
-        full_f,
-        full_f,
-        own_f,
-        own_f,
-        vm((NCB, cols, 128), F32),
-        vm((NCB, cols, 128), F32),
-        vm((NCB, cols, 128), F32),
-        vm((kt, cols, 128), BF16),
-        vm((kt, cols, 128), BF16),
-        vm((count, cols, 128), F32),
-        vm((4, cols, 128), F32),
-        vm((STAGES, NCB, cols, 128), F32),
-        vm((STAGES, nx - 1, NCB, cols, 128), F32),
-        vm((STAGES, NCB, cols, 128), BF16),
-        vm((STAGES, nz - 1, NCB, cols, 128), BF16),
-        vm((STAGES, 8, 128), F32),
-        vm((STAGES, n_plane, 8, 128), F32),
-        vm((STAGES, 8, 128), F32),
-        vm((STAGES, nz - 1, 8, 128), F32),
-        dma((5,)),
-        dma((1 + n_ex,)),
-        dma((1 + n_ex,)),
-    ] + [dma((STAGES,))] * 8
-    any_spec = pl.BlockSpec(memory_space=pl.ANY)
-    out = jax.ShapeDtypeStruct((lat, cols, 128), F32)
+    scratch = dict(
+        tab=pltpu.SMEM((8, 128), jnp.int32),
+        tabv=vm((8, 128), jnp.int32),
+        lists=vm((8, 128), jnp.int32),
+        br=vm((1, 1, count), jnp.int32),
+        bc=vm((1, 1, count), jnp.int32),
+        rs=vm((cols, lat, lon), F32),
+        co=vm((lat, lon), F32),
+        fac=vm((count, 128, 128), BF16),
+        pf=vm((lat, 128, 128), F32),
+        cf=vm(cn, F32),
+        pb=vm((lat, 128, 128), BF16),
+        pb2=vm((lat, 128, 128), BF16),
+        bmat=vm(cn, BF16),
+        bmat2=vm(cn, BF16),
+        zcat=vm((NCB, 2 * cols, 128), BF16),
+        iVO=vm((ext, rows24, 128), F32),
+        iVH=vm((ext, rows24, 128), F32),
+        isb=vm((24, rows24, 128), F32),
+        irb=vm((24, rows24, 128), F32),
+        VO=ext_f,
+        VH=ext_f,
+        sb=vm((STAGES, 24, cols, 128), F32),
+        rb=vm((STAGES, 24, cols, 128), F32),
+        LV=own_f,
+        pk=vm((2, cols, 128), F32),
+        nsb=vm((ITERS, 2 * M4 + 2, cols, 128), F32),
+        nrb=vm((ITERS, 2 * M4 + 2, cols, 128), F32),
+        pht=vm((2, 136, 128), F32),
+        phr=vm((2, 2, 136, 128), F32),
+        ph=vm((2, 128, 128), BF16),
+        ph2=vm((2, 128, 128), BF16),
+        pm=vm((2, 8, 128), F32),
+        UO=full_f,
+        UH=full_f,
+        AO=full_f,
+        AH=full_f,
+        FO=ext_f,
+        FH=ext_f,
+        c4O=vm((full, 8, 128), F32),
+        c4H=vm((full, 8, 128), F32),
+        MsO=full_f,
+        MsH=full_f,
+        TO=full_f,
+        TH=full_f,
+        xst=own_f,
+        rst=own_f,
+        S=own_f,
+        Pp=own_f,
+        yw=four,
+        xin=vm((kt, cols, 128), BF16),
+        gin=vm((kt, cols, 128), BF16),
+        run=vm((count, cols, 128), F32),
+        prev=vm((4, cols, 128), F32),
+        qa=vm((STAGES, NCB, cols, 128), F32),
+        qar=vm((STAGES, nx - 1, NCB, cols, 128), F32),
+        qb=vm((STAGES, NCB, cols, 128), BF16),
+        qbr=vm((STAGES, nz - 1, NCB, cols, 128), BF16),
+        da=vm((STAGES, 8, 128), F32),
+        dar=vm((STAGES, n_plane, 8, 128), F32),
+        db=vm((STAGES, 8, 128), F32),
+        dbr=vm((STAGES, nz - 1, 8, 128), F32),
+        insem=dma((8,)),
+        exsem_s=dma((1 + STAGES,)),
+        exsem_r=dma((1 + STAGES,)),
+        nssem_s=dma((ITERS,)),
+        nssem_r=dma((ITERS,)),
+        phsem_s=dma((2,)),
+        phsem_r=dma((2,)),
+    )
+    for name in ("qasem_s", "qasem_r", "qbsem_s", "qbsem_r", "dasem_s", "dasem_r", "dbsem_s", "dbsem_r"):
+        scratch[name] = dma((STAGES,))
+    inputs = dict(
+        picks=coarse_picks.reshape(lat),
+        br_hbm=block_rows.reshape(1, 1, count),
+        bc_hbm=block_cols.reshape(1, 1, count),
+        rs_hbm=right_side,
+        co_hbm=coeff_field,
+        f_hbm=factor_blocks.reshape(factor_blocks.shape[2:]),
+        p_hbm=prolong.reshape(lat, 128, lon),
+        c_hbm=coarse_factor.reshape(cn),
+    )
+    results = ("x_out", "r_out", "u_out")
+    out = jax.ShapeDtypeStruct((cols, lat, 128), F32)
     outs = pl.pallas_call(
-        functools.partial(kernel, cfg),
+        functools.partial(kernel, cfg, tuple(inputs) + results + tuple(scratch)),
         out_shape=(out, out, out),
-        in_specs=[pl.BlockSpec(memory_space=pltpu.SMEM)] + [any_spec] * 5,
+        in_specs=[pl.BlockSpec(memory_space=pltpu.SMEM)]
+        + [pl.BlockSpec(memory_space=pltpu.HBM)] * (len(inputs) - 1),
         out_specs=(pl.BlockSpec(memory_space=pltpu.VMEM),) * 3,
-        scratch_shapes=scratch,
+        scratch_shapes=list(scratch.values()),
         compiler_params=pltpu.CompilerParams(
-            collective_id=3, has_side_effects=True, vmem_limit_bytes=48 << 20
+            collective_id=3, has_side_effects=True, vmem_limit_bytes=63 << 20
         ),
-    )(
-        tab,
-        right_side,
-        coeff_field,
-        factor_blocks.reshape(factor_blocks.shape[2:]),
-        prolong.reshape(lat, 128, lon),
-        coarse_factor.reshape(coarse_factor.shape[1:]),
-    )
-    return tuple(jnp.transpose(value, (1, 0, 2)) for value in outs)
+    )(*inputs.values())
+
+    def hand_on(*refs):
+        for n in range(3):
+            refs[3 + n][...] = refs[n][...]
+
+    return pl.pallas_call(
+        hand_on,
+        out_shape=(out, out, out),
+    )(*outs)
 
 
 def solution(mesh):

time: 97.2 us -> 81.4 us (0.84)
  local copies, waits for them, and re-layouts: 7.18 us -> 0 us
  Pallas kernels: 86.2 us -> 80.7 us
  other arithmetic: 2.85 us -> 0 us
    unnamed x11 -> x0, local copies, waits for them, and re-layouts: 6.48 us -> none
    pallas_call x1 -> x2, Pallas kernels: 86.2 us -> 80.7 us  [the longest x1 78.7 us: local(): pl.pallas_call(functools.partial(kernel, cfg, tuple(inputs) + results + t...]
    add x2 -> x0, other arithmetic: 1.33 us -> none  [sorted_lists(): full_key = keys * 128 + at]
    reduce_sum x3 -> x0, other arithmetic: 1.29 us -> none  [the longest x1 0.95 us: sorted_lists(): last = jnp.sum((keys[None, :] <= at[:, None]).astype(jnp.int32), axis=1) - 1]
where the time goes in v2:
time: 81.4 us; the launch traced here: 81.3 us
  Pallas kernels  80.7 us (99%)
    pallas_call x1, Pallas kernels, local(): pl.pallas_call(functools.partial(kernel, cfg, tuple(inputs) + results + t...  78.7 us
    pallas_call x1, Pallas kernels, local(): return pl.pallas_call(hand_on, out_shape=(out, out, out))(*outs)  1.94 us

profile of v2, /device:TPU:1, one launch (start us, length us, event | category | flops | bytes accessed | tf_op | source)
XLA Modules:
  0.0 81.3 jit_solution(9028631867458329337)
XLA Ops:
  0.6 78.7 %shard_map.103 = (f32[16,24,128]{2,1,0:T(8,128)}, f32[16,24,128]{2,1,0:T(8,128)}, f32[16,24,128]{2,1,0:T(8,128)}) custom-call(s32[24]{0:T(128)} %bitcast.7, s32[1,1,116]{2,1,0:T(1,128)} %refs_1_.1, s32[1,1,116]{2,1,0:T(1,128)} %refs_2_.1, f32[16,24,128]{2,1,0:T(8,128)} %refs_3_.1, f32[24,128]{1,0:T(8,128)} %refs_4_.1, bf16[116,128,128]{2,1,0:T(8,128)(2,1)} %bitcast.4, ...), custom_call_target="tpu_custom_call" | custom-call | tf_op jit(solution)/shard_map/pallas_call | solution.py:859
  79.4 1.9 %shard_map.104 = (f32[16,24,128]{2,1,0:T(8,128)}, f32[16,24,128]{2,1,0:T(8,128)}, f32[16,24,128]{2,1,0:T(8,128)}) custom-call(f32[16,24,128]{2,1,0:T(8,128)} %get-tuple-element.6.refs_0_, f32[16,24,128]{2,1,0:T(8,128)} %get-tuple-element.7.refs_1_, f32[16,24,128]{2,1,0:T(8,128)} %get-tuple-element.8.refs_2_), custom_call_target="tpu_custom_call" | custom-call | tf_op jit(solution)/shard_map/pallas_call | solution.py:875

commit v3 on v2

--- a/solution.py
+++ b/solution.py
@@ -34,6 +34,10 @@
 
 def dot_nt(a, b):
     return lax.dot_general(a, b, (((1,), (1,)), ((), ())), preferred_element_type=F32)
+
+
+def far_first(count):
+    return sorted(range(1, count), key=lambda d: -min(d, count - d))
 
 
 def halves(value):
@@ -150,14 +154,14 @@
 
     def send_eight(sbe, rbe, ssem, rsem):
         for first, count, to, db_, dt_ in (
-            (0, 8, 8, -1, 0),
-            (8, 8, 0, 1, 0),
-            (16, 2, 18, 0, 1),
-            (18, 2, 16, 0, -1),
             (16, 1, 22, -1, 1),
             (17, 1, 20, 1, 1),
             (18, 1, 23, -1, -1),
             (19, 1, 21, 1, -1),
+            (16, 2, 18, 0, 1),
+            (18, 2, 16, 0, -1),
+            (0, 8, 8, -1, 0),
+            (8, 8, 0, 1, 0),
         ):
             pltpu.make_async_remote_copy(
                 src_ref=sbe.at[pl.ds(first, count)],
@@ -235,13 +239,13 @@
         return loop(count, body, acc, unroll=count)
 
     def send_x(k):
-        for d in range(nx - 1):
+        for d in far_first(nx):
             pltpu.make_async_remote_copy(
                 src_ref=qa.at[k],
-                dst_ref=qar.at[k, d],
+                dst_ref=qar.at[k, d - 1],
                 send_sem=qasem_s.at[k],
                 recv_sem=qasem_r.at[k],
-                device_id=x_peer(d + 1),
+                device_id=x_peer(d),
                 device_id_type=MESH,
             ).start()
 
@@ -265,7 +269,12 @@
                 device_id_type=MESH,
             ).start()
 
-        loop(n_plane, send)
+        def hops(d):
+            dy, dx = (d // nx) // 2, d % nx
+            return min(dy, n_b // 2 - dy) + min(dx, nx - dx)
+
+        for d in sorted(range(1, n_plane + 1), key=lambda d: -hops(d)):
+            send(d - 1)
 
     def reduce_mid(k):
         pltpu.make_async_copy(qar.at[k], qar.at[k], qasem_r.at[k]).wait()
@@ -285,8 +294,8 @@
                 device_id_type=MESH,
             ).start()
 
-        for d in range(nz - 1):
-            send_q(d)
+        for d in far_first(nz):
+            send_q(d - 1)
 
     def dots_mid(k):
         pltpu.make_async_copy(dar.at[k], dar.at[k], dasem_r.at[k]).wait()
@@ -305,8 +314,8 @@
                 device_id_type=MESH,
             ).start()
 
-        for d in range(nz - 1):
-            send_d(d)
+        for d in far_first(nz):
+            send_d(d - 1)
 
     def reduce_end(k):
         pltpu.make_async_copy(qbr.at[k], qbr.at[k], qbsem_r.at[k]).wait()
@@ -325,7 +334,7 @@
         shape = (cols, 128)
         return tuple(jnp.broadcast_to(tile[:, n : n + 1], shape) for n in range(3))
 
-    def local_solve():
+    def local_solve(between):
         lane = lane_of(cols)
         zero = jnp.zeros((cols, 128), F32)
 
@@ -358,6 +367,7 @@
             return acc
 
         loop(nb_blocks, outer, zero, unroll=nb_blocks)
+        between()
 
         def unflatten(j, carry):
             s = 4 * j + W
@@ -471,16 +481,6 @@
     pl.semaphore_wait(barrier, n_plane + nz - 1 + 6)
     send_eight(isb, irb, exsem_s.at[0], exsem_r.at[0])
     send_x(0)
-    for n, d in enumerate((1, -1)):
-        pltpu.make_async_remote_copy(
-            src_ref=pht,
-            dst_ref=phr.at[n],
-            send_sem=phsem_s.at[n],
-            recv_sem=phsem_r.at[n],
-            device_id=(b, tile_at(d)),
-            device_id_type=MESH,
-        ).start()
-
     loads[5].wait()
     for m in range(NCB):
         value = lax.dot_general(
@@ -514,6 +514,17 @@
         c4H[i] = (h[cols:rows24] + 4.0) * (side * inside)
 
     assemble(iVO, isb, irb, exsem_r.at[0], take_first)
+    for n, d in enumerate((1, -1)):
+        pltpu.make_async_remote_copy(
+            src_ref=pht,
+            dst_ref=phr.at[n],
+            send_sem=phsem_s.at[n],
+            recv_sem=phsem_r.at[n],
+            device_id=(b, tile_at(d)),
+            device_id_type=MESH,
+        ).start()
+
+    reduce_mid(0)
     loads[6].wait()
     to_smem.wait()
 
@@ -569,9 +580,18 @@
 
         loop(count, body, unroll=count)
 
+    def leave(n):
+        return pltpu.make_async_copy(
+            r[("xst2", "rst2", "ust")[n]], r[("x_out", "r_out", "u_out")[n]], r["outsem"].at[n]
+        )
+
     def stage(k, carry):
-        local_solve()
-        reduce_mid(k)
+        def between():
+            @pl.when(k > 0)
+            def _():
+                reduce_mid(k)
+
+        local_solve(between)
         pack(VO, VH, sb.at[k])
         send_eight(sb.at[k], rb.at[k], exsem_s.at[1 + k], exsem_r.at[1 + k])
 
@@ -591,11 +611,6 @@
                 ph2[half] = (value - high.astype(F32)).astype(BF16)
                 pm[half] = jnp.where(from_west[0:8], phr[0, half, 128:136], phr[1, half, 128:136])
 
-        def keep(i, o, h):
-            TO[i] = o
-            TH[i] = h
-
-        assemble(VO, sb.at[k], rb.at[k], exsem_r.at[1 + k], keep)
         reduce_end(k)
 
         solved = jnp.zeros((cols, NCB * 128), F32)
@@ -636,6 +651,12 @@
 
         lift(M4, own - 2 * M4)
 
+        def keep(i, o, h):
+            TO[i] = o
+            TH[i] = h
+
+        assemble(VO, sb.at[k], rb.at[k], exsem_r.at[1 + k], keep)
+
         @pl.when(k > 0)
         def _():
             g, d, e = dots_end(k)
@@ -656,6 +677,16 @@
                 r_out[row] = r_out[row] - alpha * s
 
             loop(own, body, unroll=own)
+
+        @pl.when(k == STAGES - 1)
+        def _():
+            def body(row):
+                r["xst2"][:, row, :] = x_out[row]
+                r["rst2"][:, row, :] = r_out[row]
+
+            loop(own, body, unroll=own)
+            leave(0).start()
+            leave(1).start()
 
         alpha = prev[2]
         beta = prev[3]
@@ -717,11 +748,10 @@
         @pl.when(k == STAGES - 1)
         def _():
             def body(row):
-                r["x_out"][:, row, :] = x_out[row]
-                r["r_out"][:, row, :] = r_out[row]
-                r["u_out"][:, row, :] = UO[row + M4]
+                r["ust"][:, row, :] = UO[row + M4]
 
             loop(own, body, unroll=own)
+            leave(2).start()
 
         return carry
 
@@ -752,6 +782,8 @@
         pltpu.make_async_copy(dbr.at[k + 1], dbr.at[k + 1], dbsem_s.at[k + 1]).wait()
 
     loop(STAGES - 1, sent_d)
+    for n in range(3):
+        leave(n).wait()
 
 
 def local(n_b, n_t, right_side, coeff_field, factor_blocks, block_rows, block_cols, prolong, coarse_picks, coarse_factor):
@@ -817,6 +849,10 @@
         MsH=full_f,
         TO=full_f,
         TH=full_f,
+        xst2=vm((cols, lat, 128), F32),
+        rst2=vm((cols, lat, 128), F32),
+        ust=vm((cols, lat, 128), F32),
+        outsem=dma((3,)),
         xst=own_f,
         rst=own_f,
         S=own_f,
@@ -861,7 +897,7 @@
         out_shape=(out, out, out),
         in_specs=[pl.BlockSpec(memory_space=pltpu.SMEM)]
         + [pl.BlockSpec(memory_space=pltpu.HBM)] * (len(inputs) - 1),
-        out_specs=(pl.BlockSpec(memory_space=pltpu.VMEM),) * 3,
+        out_specs=(pl.BlockSpec(memory_space=pltpu.HBM),) * 3,
         scratch_shapes=list(scratch.values()),
         compiler_params=pltpu.CompilerParams(
             collective_id=3, has_side_effects=True, vmem_limit_bytes=63 << 20

time: 81.4 us -> 72.8 us (0.89)
  Pallas kernels: 80.7 us -> 72.1 us
    pallas_call x1, Pallas kernels: 78.7 us -> 70.2 us  [local(): pl.pallas_call(functools.partial(kernel, cfg, tuple(inputs) + results + t...]
where the time goes in v3:
time: 72.8 us; the launch traced here: 72.7 us
  Pallas kernels  72.1 us (99%)
    pallas_call x1, Pallas kernels, local(): pl.pallas_call(functools.partial(kernel, cfg, tuple(inputs) + results + t...  70.2 us
    pallas_call x1, Pallas kernels, local(): return pl.pallas_call(hand_on, out_shape=(out, out, out))(*outs)  1.94 us

profile of v3, /device:TPU:1, one launch (start us, length us, event | category | flops | bytes accessed | tf_op | source)
XLA Modules:
  0.0 72.7 jit_solution(8594772618113034942)
XLA Ops:
  0.6 70.2 %shard_map.103 = (f32[16,24,128]{2,1,0:T(8,128)}, f32[16,24,128]{2,1,0:T(8,128)}, f32[16,24,128]{2,1,0:T(8,128)}) custom-call(s32[24]{0:T(128)} %bitcast.7, s32[1,1,116]{2,1,0:T(1,128)} %refs_1_.1, s32[1,1,116]{2,1,0:T(1,128)} %refs_2_.1, f32[16,24,128]{2,1,0:T(8,128)} %refs_3_.1, f32[24,128]{1,0:T(8,128)} %refs_4_.1, bf16[116,128,128]{2,1,0:T(8,128)(2,1)} %bitcast.4, ...), custom_call_target="tpu_custom_call" | custom-call | tf_op jit(solution)/shard_map/pallas_call | solution.py:895
  70.8 1.9 %shard_map.104 = (f32[16,24,128]{2,1,0:T(8,128)}, f32[16,24,128]{2,1,0:T(8,128)}, f32[16,24,128]{2,1,0:T(8,128)}) custom-call(f32[16,24,128]{2,1,0:T(8,128)} %get-tuple-element.6.refs_0_, f32[16,24,128]{2,1,0:T(8,128)} %get-tuple-element.7.refs_1_, f32[16,24,128]{2,1,0:T(8,128)} %get-tuple-element.8.refs_2_), custom_call_target="tpu_custom_call" | custom-call | tf_op jit(solution)/shard_map/pallas_call | solution.py:911

commit v4 on v3

--- a/solution.py
+++ b/solution.py
@@ -52,8 +52,10 @@
     x_out, r_out = r["xst"], r["rst"]
     picks, tab, tabv, lists = r["picks"], r["tab"], r["tabv"], r["lists"]
     rs, co, fac, pf, cf = r["rs"], r["co"], r["fac"], r["pf"], r["cf"]
+    facT = r["facT"]
     pb, pb2, bmat, bmat2, zcat = r["pb"], r["pb2"], r["bmat"], r["bmat2"], r["zcat"]
     iVO, iVH, isb, irb = r["iVO"], r["iVH"], r["isb"], r["irb"]
+    cVO, cVH, csb, crb = r["cVO"], r["cVH"], r["csb"], r["crb"]
     VO, VH, sb, rb = r["VO"], r["VH"], r["sb"], r["rb"]
     LV, pk, nsb, nrb = r["LV"], r["pk"], r["nsb"], r["nrb"]
     pht, phr, ph, ph2, pm = r["pht"], r["phr"], r["ph"], r["ph2"], r["pm"]
@@ -78,35 +80,42 @@
     sources = (r["br_hbm"], r["bc_hbm"], rs_hbm, co_hbm, p_hbm, c_hbm, f_hbm)
     targets = (r["br"], r["bc"], rs, co, pf, cf, fac)
     loads = [pltpu.make_async_copy(a, c, insem.at[n]) for n, (a, c) in enumerate(zip(sources, targets))]
+    bands = [lax.rem(b + d, n_b) for d in range(n_b)]
+    tiles_x = [z * nx + lax.rem(x + d, nx) for d in range(nx)]
+    tiles_z = [lax.rem(t + nx * d, n_t) for d in range(nz)]
+    tiles_next = {1: lax.rem(t + 1, n_t), -1: lax.rem(t + n_t - 1, n_t), 0: t}
+
+    def band_at(d):
+        return bands[d % n_b]
+
+    def tile_at(d):
+        return tiles_next[d]
+
+    def x_peer(d):
+        return (b, tiles_x[d])
+
+    def z_peer(d):
+        return (b, tiles_z[d])
+
+    def plane_peer(d):
+        return (bands[d // nx], tiles_x[d % nx])
+
+    n_plane = n_b * nx - 1
+    barrier = pltpu.get_barrier_semaphore()
+
+    def greet(device):
+        pl.semaphore_signal(barrier, inc=1, device_id=device, device_id_type=MESH)
+
     for copy in loads:
         copy.start()
-
-    def band_at(d):
-        return lax.rem(b + d + n_b, n_b)
-
-    def tile_at(d):
-        return lax.rem(t + d + n_t, n_t)
-
-    def x_peer(d):
-        return (b, z * nx + lax.rem(x + d, nx))
-
-    def z_peer(d):
-        return (b, lax.rem(t + nx * d, n_t))
-
-    def plane_peer(d):
-        return (lax.rem(b + d // nx, n_b), z * nx + lax.rem(x + lax.rem(d, nx), nx))
-
-    n_plane = n_b * nx - 1
-    barrier = pltpu.get_barrier_semaphore()
-
-    def greet(device):
-        pl.semaphore_signal(barrier, inc=1, device_id=device, device_id_type=MESH)
-
-    loop(n_plane, lambda d: greet(plane_peer(d + 1)))
-    loop(nz - 1, lambda d: greet(z_peer(d + 1)))
+    for d in range(1, n_plane + 1):
+        greet(plane_peer(d))
+    for d in far_first(nz):
+        greet(z_peer(d))
     for db_ in (-1, 0, 1):
         for dt_ in (-1, 1):
             greet((band_at(db_), tile_at(dt_)))
+
 
     has_n = (b > 0).astype(F32)
     has_s = (b < n_b - 1).astype(F32)
@@ -279,9 +288,9 @@
     def reduce_mid(k):
         pltpu.make_async_copy(qar.at[k], qar.at[k], qasem_r.at[k]).wait()
         for m in range(NCB):
-            total = qa[k, m]
+            total = qa[k, m].astype(F32)
             for d in range(nx - 1):
-                total = total + qar[k, d, m]
+                total = total + qar[k, d, m].astype(F32)
             qb[k, m] = total.astype(BF16)
 
         def send_q(d):
@@ -350,7 +359,7 @@
         xin[ext] = tail.astype(BF16)
 
         def inner(n, acc):
-            acc = acc * tab[2, n].astype(F32) + dot_nt(xin[tab[1, n]], fac[tab[0, n]])
+            acc = acc * tab[2, n].astype(F32) + dot_nn(xin[tab[1, n]], facT[tab[0, n]])
             run[n] = acc
             return acc
 
@@ -366,8 +375,10 @@
             run[n] = acc
             return acc
 
-        loop(nb_blocks, outer, zero, unroll=nb_blocks)
+        early = nb_blocks * 5 // 8
+        acc = loop(early, outer, zero, unroll=early)
         between()
+        loop(nb_blocks - early, lambda n, a: outer(early + n, a), acc, unroll=nb_blocks - early)
 
         def unflatten(j, carry):
             s = 4 * j + W
@@ -421,14 +432,12 @@
     to_smem = pltpu.make_async_copy(tabv, tab, insem.at[7])
     to_smem.start()
 
-    rows24 = cols + 8
-    zero24 = jnp.zeros((rows24, 128), F32)
     zero = jnp.zeros((cols, 128), F32)
     lane16 = lane_of(cols)
     for row in (0, 1, ext - 2, ext - 1):
-        iVO[row] = zero24
-    iVH[...] = jnp.zeros(iVH.shape, F32)
-    for ref in (UO, UH, MsO, MsH, S, Pp):
+        iVO[row] = zero
+        cVO[row] = zero[0:8]
+    for ref in (iVH, cVH, UO, UH, MsO, MsH, S, Pp):
         ref[...] = jnp.zeros(ref.shape, F32)
     prev[...] = jnp.ones(prev.shape, F32)
     prev[2] = jnp.full((cols, 128), -1.0, F32)
@@ -441,9 +450,10 @@
         r_out[row] = value
         FO[row + W] = value
         x_out[row] = zero
-        iVO[W + row, 0:cols] = value
-        iVO[W + row, cols:rows24] = jnp.broadcast_to(co[row : row + 1, :], (8, 128))
+        iVO[W + row] = value
+        cVO[W + row] = jnp.broadcast_to(co[row : row + 1, :], (8, 128))
     pack(iVO, iVH, isb)
+    pack(cVO, cVH, csb)
 
     loads[4].wait()
 
@@ -456,7 +466,7 @@
     loop(own, to_bf16, unroll=4)
     acc = restrict(0, own, (zero,) * NCB)
     for m in range(NCB):
-        qa[0, m] = acc[m]
+        qa[0, m] = acc[m].astype(BF16)
 
     group128 = lane128 // 8
     group8 = group128[0:8]
@@ -481,6 +491,13 @@
     pl.semaphore_wait(barrier, n_plane + nz - 1 + 6)
     send_eight(isb, irb, exsem_s.at[0], exsem_r.at[0])
     send_x(0)
+    send_eight(csb, crb, exsem_s.at[1 + STAGES], exsem_r.at[1 + STAGES])
+    loads[6].wait()
+
+    def turned(n):
+        facT[n] = jnp.transpose(fac[n])
+
+    loop(nb_blocks, turned, unroll=4)
     loads[5].wait()
     for m in range(NCB):
         value = lax.dot_general(
@@ -500,8 +517,10 @@
         else:
             keep = True
         if keep:
-            FO[i - W] = o[0:cols]
-            FH[i - W] = near(h[0:cols])
+            FO[i - W] = o
+            FH[i - W] = near(h)
+
+    def take_coefficients(i, o, h):
         inside = 0.25
         if isinstance(i, int):
             if i < M4:
@@ -510,8 +529,8 @@
                 inside = 0.25 * has_s
         lane8 = lane16[0:8]
         side = jnp.where(lane8 >= 128 - M4, has_w, 0.0) + jnp.where(lane8 < M4, has_e, 0.0)
-        c4O[i] = (o[cols:rows24] + 4.0) * inside
-        c4H[i] = (h[cols:rows24] + 4.0) * (side * inside)
+        c4O[i] = (o + 4.0) * inside
+        c4H[i] = (h + 4.0) * (side * inside)
 
     assemble(iVO, isb, irb, exsem_r.at[0], take_first)
     for n, d in enumerate((1, -1)):
@@ -525,7 +544,6 @@
         ).start()
 
     reduce_mid(0)
-    loads[6].wait()
     to_smem.wait()
 
     side16 = jnp.where(lane16 >= 128 - M4, has_w, 0.0) + jnp.where(lane16 < M4, has_e, 0.0)
@@ -610,6 +628,7 @@
                 ph[half] = high
                 ph2[half] = (value - high.astype(F32)).astype(BF16)
                 pm[half] = jnp.where(from_west[0:8], phr[0, half, 128:136], phr[1, half, 128:136])
+            assemble(cVO, csb, crb, exsem_r.at[1 + STAGES], take_coefficients)
 
         reduce_end(k)
 
@@ -715,6 +734,16 @@
             loop(full - 12, lambda n: twice(6 + n), unroll=full - 12)
             acc = restrict(2, own - 4, (zero,) * NCB)
 
+            def dots(row, sums):
+                u = UO[row + M4]
+                return (
+                    sums[0] + u * r_out[row],
+                    sums[1] + u * FO[row + W],
+                    sums[2] + u * S[row],
+                )
+
+            sums = loop(own - 4, lambda n, a: dots(2 + n, a), (zero, zero, zero), unroll=own - 4)
+
             pltpu.make_async_copy(nrb.at[k], nrb.at[k], nssem_r.at[k]).wait()
             for n in range(M4):
                 combine(n, nrb[k, n] * has_n, pltpu.roll(nrb[k, M4], 60 - 8 * n, 1) * (has_n * side16))
@@ -732,18 +761,12 @@
             acc = restrict(0, 2, acc)
             acc = restrict(own - 2, 2, acc)
             for m in range(NCB):
-                qa[k + 1, m] = acc[m]
+                qa[k + 1, m] = acc[m].astype(BF16)
             send_x(k + 1)
 
-            def dots(row, acc):
-                u = UO[row + M4]
-                return (
-                    acc[0] + u * r_out[row],
-                    acc[1] + u * FO[row + W],
-                    acc[2] + u * S[row],
-                )
-
-            dots_send(k + 1, *loop(own, dots, (zero, zero, zero), unroll=own))
+            for row in (0, 1, own - 2, own - 1):
+                sums = dots(row, sums)
+            dots_send(k + 1, *sums)
 
         @pl.when(k == STAGES - 1)
         def _():
@@ -758,6 +781,7 @@
     lax.fori_loop(0, STAGES, stage, 0)
 
     pltpu.make_async_copy(irb, irb, exsem_s.at[0]).wait()
+    pltpu.make_async_copy(crb, crb, exsem_s.at[1 + STAGES]).wait()
 
     def sent(e):
         pltpu.make_async_copy(rb.at[e], rb.at[e], exsem_s.at[1 + e]).wait()
@@ -796,7 +820,6 @@
     nz = n_t // nx
     cfg = (n_b, n_t, nx, nz, lat, count, kt, cols)
     n_plane = n_b * nx - 1
-    rows24 = cols + 8
     vm = pltpu.VMEM
     ext_f = vm((ext, cols, 128), F32)
     full_f = vm((full, cols, 128), F32)
@@ -813,6 +836,7 @@
         rs=vm((cols, lat, lon), F32),
         co=vm((lat, lon), F32),
         fac=vm((count, 128, 128), BF16),
+        facT=vm((count, 128, 128), BF16),
         pf=vm((lat, 128, 128), F32),
         cf=vm(cn, F32),
         pb=vm((lat, 128, 128), BF16),
@@ -820,10 +844,14 @@
         bmat=vm(cn, BF16),
         bmat2=vm(cn, BF16),
         zcat=vm((NCB, 2 * cols, 128), BF16),
-        iVO=vm((ext, rows24, 128), F32),
-        iVH=vm((ext, rows24, 128), F32),
-        isb=vm((24, rows24, 128), F32),
-        irb=vm((24, rows24, 128), F32),
+        iVO=ext_f,
+        iVH=ext_f,
+        isb=vm((24, cols, 128), F32),
+        irb=vm((24, cols, 128), F32),
+        cVO=vm((ext, 8, 128), F32),
+        cVH=vm((ext, 8, 128), F32),
+        csb=vm((24, 8, 128), F32),
+        crb=vm((24, 8, 128), F32),
         VO=ext_f,
         VH=ext_f,
         sb=vm((STAGES, 24, cols, 128), F32),
@@ -862,8 +890,8 @@
         gin=vm((kt, cols, 128), BF16),
         run=vm((count, cols, 128), F32),
         prev=vm((4, cols, 128), F32),
-        qa=vm((STAGES, NCB, cols, 128), F32),
-        qar=vm((STAGES, nx - 1, NCB, cols, 128), F32),
+        qa=vm((STAGES, NCB, cols, 128), BF16),
+        qar=vm((STAGES, nx - 1, NCB, cols, 128), BF16),
         qb=vm((STAGES, NCB, cols, 128), BF16),
         qbr=vm((STAGES, nz - 1, NCB, cols, 128), BF16),
         da=vm((STAGES, 8, 128), F32),
@@ -871,8 +899,8 @@
         db=vm((STAGES, 8, 128), F32),
         dbr=vm((STAGES, nz - 1, 8, 128), F32),
         insem=dma((8,)),
-        exsem_s=dma((1 + STAGES,)),
-        exsem_r=dma((1 + STAGES,)),
+        exsem_s=dma((2 + STAGES,)),
+        exsem_r=dma((2 + STAGES,)),
         nssem_s=dma((ITERS,)),
         nssem_r=dma((ITERS,)),
         phsem_s=dma((2,)),
@@ -905,12 +933,25 @@
     )(*inputs.values())
 
     def hand_on(*refs):
+        sems = refs[9]
+        into = [pltpu.make_async_copy(refs[n], refs[6 + n], sems.at[n]) for n in range(3)]
+        onto = [pltpu.make_async_copy(refs[6 + n], refs[3 + n], sems.at[3 + n]) for n in range(3)]
+        for copy in into:
+            copy.start()
         for n in range(3):
-            refs[3 + n][...] = refs[n][...]
-
+            into[n].wait()
+            onto[n].start()
+        for copy in onto:
+            copy.wait()
+
+    hbm = pl.BlockSpec(memory_space=pltpu.HBM)
     return pl.pallas_call(
         hand_on,
         out_shape=(out, out, out),
+        in_specs=[hbm] * 3,
+        out_specs=(hbm,) * 3,
+        scratch_shapes=[vm(out.shape, F32)] * 3 + [dma((6,))],
+        compiler_params=pltpu.CompilerParams(vmem_limit_bytes=63 << 20),
     )(*outs)
 
 

time: 72.8 us -> 70.1 us (0.963)
  Pallas kernels: 72.1 us -> 69.3 us
    pallas_call x1, Pallas kernels: 70.2 us -> 67.4 us  [local(): pl.pallas_call(functools.partial(kernel, cfg, tuple(inputs) + results + t...]
where the time goes in v4:
time: 70.1 us; the launch traced here: 69.9 us
  Pallas kernels  69.3 us (99%)
    pallas_call x1, Pallas kernels, local(): pl.pallas_call(functools.partial(kernel, cfg, tuple(inputs) + results + t...  67.4 us
    pallas_call x1, Pallas kernels, local(): pl.pallas_call(hand_on, out_shape=(out, out, out), in_specs=[hbm] * 3, ou...  1.84 us

profile of v4, /device:TPU:1, one launch (start us, length us, event | category | flops | bytes accessed | tf_op | source)
XLA Modules:
  0.0 69.9 jit_solution(16069977510776873458)
XLA Ops:
  0.6 67.4 %shard_map.103 = (f32[16,24,128]{2,1,0:T(8,128)}, f32[16,24,128]{2,1,0:T(8,128)}, f32[16,24,128]{2,1,0:T(8,128)}) custom-call(s32[24]{0:T(128)} %bitcast.7, s32[1,1,116]{2,1,0:T(1,128)} %refs_1_.1, s32[1,1,116]{2,1,0:T(1,128)} %refs_2_.1, f32[16,24,128]{2,1,0:T(8,128)} %refs_3_.1, f32[24,128]{1,0:T(8,128)} %refs_4_.1, bf16[116,128,128]{2,1,0:T(8,128)(2,1)} %bitcast.4, ...), custom_call_target="tpu_custom_call" | custom-call | tf_op jit(solution)/shard_map/pallas_call | solution.py:923
  68.1 1.8 %shard_map.104 = (f32[16,24,128]{2,1,0:T(8,128)}, f32[16,24,128]{2,1,0:T(8,128)}, f32[16,24,128]{2,1,0:T(8,128)}) custom-call(f32[16,24,128]{2,1,0:T(8,128)} %get-tuple-element.6.refs_0_, f32[16,24,128]{2,1,0:T(8,128)} %get-tuple-element.7.refs_1_, f32[16,24,128]{2,1,0:T(8,128)} %get-tuple-element.8.refs_2_), custom_call_target="tpu_custom_call" | custom-call | tf_op jit(solution)/shard_map/pallas_call | solution.py:948
